TPU v7x, 32 devices: a whole 2x2x4 slice. The times are simulated.
32 devices in a mesh: ex: 2 (over core), slab: 16 (over z, y, x).
Axes of the slice: x: 2, y: 2, z: 4, core: 2. Of those that a mesh axis runs over, the one named last changes fastest.
Arguments:
- volume: bfloat16 [2, 16, 128, 32, 128], P('ex', None, 'slab'), may hold values from -6 to 6
- cotangent: bfloat16 [2, 16, 128, 32, 128], P('ex', None, 'slab')
- gate_mask: int32 [2, 2, 128, 32, 128], P('ex', None, 'slab'), may hold values 0 or 1
- loss_scale: float32 [2], P('ex'), may hold values from 0.05 to 5
- canary: int32 [2], P('ex'), may hold values from 0 to 15
- kernels: bfloat16 [2, 32, 432], replicated, may hold values from -0.3125 to 0.3125
Outputs:
- input_grad: float32 [2, 16, 128, 32, 128], P('ex', None, 'slab')
- kernel_grad: float32 [2, 32, 432], replicated
All inputs are finite; a program needn't handle non-finite values. No bound on the sum of `gate_mask` on one device may be relied on, other than what follows from the above.
Results may differ from a plain program's by a relative error of at most 0.0037.
Values may be sent and summed in bfloat16 or wider, within the bound.
No kernel may reach another device: no remote copies, remote signals or barrier semaphores. Data moves between devices by JAX's collectives and lax.ppermute only.
A program may use at most 192 MiB of HBM per device.

v0:
```python
import jax
import jax.numpy as jnp
from jax import lax
from jax.sharding import PartitionSpec as P


def with_halo(array, sides, width):
    for axis, dim in sides:
        peers, length = (lax.axis_size(axis), array.shape[dim])
        up = [(i, (i + 1) % peers) for i in range(peers - 1)]
        down = [(j, i) for i, j in up]
        last = lax.slice_in_dim(array, length - width, length, axis=dim)
        leading = lax.slice_in_dim(array, 0, width, axis=dim)
        before = lax.ppermute(last, axis, up)
        after = lax.ppermute(leading, axis, down)
        array = jnp.concatenate([before, array, after], axis=dim)
    return array


def columns(extended):
    zs = extended.shape[2] - 2
    hs, ws = (extended.shape[3], extended.shape[4])
    padded = jnp.pad(extended, ((0, 0), (0, 0), (0, 0), (1, 1), (1, 1)))
    taps = []
    for dz in range(3):
        for dh in range(3):
            for dw in range(3):
                taps.append(padded[:, :, dz : dz + zs, dh : dh + hs, dw : dw + ws])
    stacked = jnp.stack(taps, axis=1)
    return stacked.reshape((extended.shape[0], 27 * extended.shape[1], zs, hs, ws))


def back_columns(extended):
    zs = extended.shape[2] - 2
    hs, ws = (extended.shape[3], extended.shape[4])
    padded = jnp.pad(extended, ((0, 0), (0, 0), (0, 0), (1, 1), (1, 1)))
    taps = []
    for dz in range(3):
        for dh in range(3):
            for dw in range(3):
                taps.append(
                    padded[:, :, 2 - dz : 2 - dz + zs, 2 - dh : 2 - dh + hs, 2 - dw : 2 - dw + ws]
                )
    return jnp.stack(taps, axis=1)


def layer_forward(field, kernel):
    extended = with_halo(field, (("slab", 2),), 1)
    patches = columns(extended)
    pre = jnp.einsum("ok,ekzhw->eozhw", kernel, patches, preferred_element_type=jnp.float32)
    return (pre, patches)


def layer_backward(delta, kernel, patches):
    grads = jnp.einsum("eozhw,ekzhw->eok", delta, patches, preferred_element_type=jnp.float32)
    extended = with_halo(delta, (("slab", 2),), 1)
    width = kernel.shape[1] // 27
    shaped = kernel.reshape((kernel.shape[0], 27, width))
    spread = jnp.einsum(
        "otc,etozhw->eczhw", shaped, back_columns(extended), preferred_element_type=jnp.float32
    )
    return (grads, spread)


def per_device(volume, cotangent, gate_mask, loss_scale, canary, kernels):
    chans = volume.shape[1]
    local_ex = volume.shape[0]
    mask_one = gate_mask[:, 0][:, None].astype(jnp.float32)
    mask_two = gate_mask[:, 1][:, None].astype(jnp.float32)
    pre_one, patches_one = layer_forward(volume, kernels[0])
    value_one = pre_one[:, :chans]
    sig_one = jax.nn.sigmoid(pre_one[:, chans:])
    hidden = (volume.astype(jnp.float32) + value_one * sig_one * mask_one).astype(jnp.bfloat16)
    pre_two, patches_two = layer_forward(hidden, kernels[1])
    value_two = pre_two[:, :chans]
    sig_two = jax.nn.sigmoid(pre_two[:, chans:])
    channel_ids = jnp.arange(chans, dtype=jnp.int32)
    weights = 1.0 + 2.0 * (channel_ids[None, :] == canary[:, None]).astype(jnp.float32)
    weights = weights * loss_scale[:, None]
    grad_out = cotangent.astype(jnp.float32) * weights[:, :, None, None, None]
    delta_two = jnp.concatenate(
        [
            grad_out * sig_two * mask_two,
            grad_out * value_two * sig_two * (1.0 - sig_two) * mask_two,
        ],
        axis=1,
    ).astype(jnp.bfloat16)
    grad_two, spread_two = layer_backward(delta_two, kernels[1], patches_two)
    grad_hidden = grad_out + spread_two
    delta_one = jnp.concatenate(
        [
            grad_hidden * sig_one * mask_one,
            grad_hidden * value_one * sig_one * (1.0 - sig_one) * mask_one,
        ],
        axis=1,
    ).astype(jnp.bfloat16)
    grad_one, spread_one = layer_backward(delta_one, kernels[0], patches_one)
    input_grad = grad_hidden + spread_one
    stacked = jnp.stack([grad_one, grad_two], axis=1)
    flat = stacked.reshape((local_ex, -1))
    depth = volume.shape[2] * lax.axis_size("slab")
    bound = 20.0 * jnp.sqrt(jnp.float32(depth * volume.shape[3] * volume.shape[4]))
    examples = local_ex * lax.axis_size("ex")
    scaling = jnp.sqrt(jnp.float32(108 * chans * chans)) / (bound * jnp.sqrt(jnp.float32(examples)))
    summed = lax.psum(flat, "slab")
    norm = jnp.sqrt(jnp.sum(summed * summed, axis=1) + 1e-06)
    factor = jnp.minimum(1.0, bound / norm)
    local_total = jnp.sum(summed * factor[:, None], axis=0)
    total = lax.psum(local_total, "ex")
    kernel_grad = (total * scaling).reshape(kernels.shape)
    return (input_grad, kernel_grad)


def solution(mesh):
    placed = (
        P("ex", None, "slab", None, None),
        P("ex", None, "slab", None, None),
        P("ex", None, "slab", None, None),
        P("ex"),
        P("ex"),
        P(),
    )
    return jax.shard_map(
        per_device,
        mesh=mesh,
        in_specs=placed,
        out_specs=(P("ex", None, "slab", None, None), P()),
        check_vma=False,
    )
```

profile of v0, /device:TPU:0, one launch (start us, length us, event | category | flops | bytes accessed | tf_op | source)
XLA Modules:
  0.0 632.6 jit_solution(10339286608299501109)
XLA Ops:
  8.2 4.8 collective-permute-start
  15.8 4.8 collective-permute-done.1
  20.6 3.8 select_maximum_fusion.5
  31.1 2.2 fusion.160
  34.9 2.2 fusion.158
  37.1 2.2 fusion.157
  46.1 2.3 fusion.152
  49.9 2.2 fusion.150
  52.1 2.3 fusion.149
  61.4 2.2 fusion.142
  65.2 2.3 fusion.140
  67.5 2.2 fusion.139
  69.8 26.2 %copy.22 = bf16[1,27,16,8,32,128]{5,2,1,4,3,0:T(8,128)(2,1)} copy(bf16[1,27,16,8,32,128]{5,4,3,2,1,0:T(8,128)(2,1)} %fusion.139) | data formatting | bytes 56623104 | tf_op jit(solution)/shard_map/stack | solution.py:29
  95.9 11.7 %convolution_bitcast_fusion = f32[1,32,8,32,128]{4,1,3,2,0:T(8,128)S(1)} fusion(bf16[432,8,32,128]{3,0,2,1:T(8,128)(2,1)} %bitcast.515, bf16[2,32,432]{2,1,0:T(8,128)(2,1)S(1)} %copy-done.4), kind=kOutput, calls=%fused_computation.52 | convolution fusion | flops 905969664 | bytes 32538624 | tf_op jit(solution)/shard_map/ok,ekzhw->eozhw/dot_general | solution.py:50
  110.9 3.7 collective-permute-start.2
  118.5 2.9 collective-permute-done.3
  121.4 2.2 select_maximum_fusion.7
  158.4 19.5 %copy.23 = bf16[1,27,16,8,32,128]{5,4,3,2,1,0:T(8,128)(2,1)} copy(bf16[1,27,16,8,32,128]{5,2,4,3,1,0:T(8,128)(2,1)} %fusion.111) | data formatting | bytes 56623104 | tf_op jit(solution)/shard_map/stack | solution.py:29
  177.9 28.2 %fusion.30 = f32[1,32,8,32,128]{4,1,3,2,0:T(8,128)S(1)} fusion(bf16[432,8,32,128]{3,2,1,0:T(8,128)(2,1)} %bitcast.513, bf16[2,32,432]{2,1,0:T(8,128)(2,1)S(1)} %copy-done.4), kind=kOutput, calls=%fused_computation.51 | convolution fusion | flops 905969664 | bytes 32538624 | tf_op jit(solution)/shard_map/ok,ekzhw->eozhw/dot_general | solution.py:50
  208.3 4.0 collective-permute-start.4
  213.6 48.5 %fusion.101 = f32[1,1,32,432]{3,2,1,0:T(8,128)} fusion(bf16[432,8,32,128]{3,2,1,0:T(8,128)(2,1)} %bitcast.514, bf16[16,8,32,128]{3,0,2,1:T(8,128)(2,1)S(1)} %bitcast.522, bf16[16,8,32,128]{3,0,2,1:T(8,128)(2,1)S(1)} %bitcast.520), kind=kOutput, calls=%fused_computation.191 | convolution fusion | flops 910163968 | bytes 30464000 | tf_op jit(solution)/shard_map/eozhw,ekzhw->eok/dot_general | solution.py:55
  262.2 6.8 %select_maximum_fusion.3 = bf16[1,32,10,34,130]{4,1,3,2,0:T(8,128)(2,1)S(1)} fusion(bf16[1,32,1,32,128]{4,1,3,2,0:T(8,128)(2,1)} %collective-permute-done.5, bf16[1,32,1,32,128]{4,1,3,2,0:T(8,128)(2,1)S(1)} %collective-permute-done.4, bf16[1,16,8,32,128]{4,1,3,2,0:T(8,128)(2,1)S(1)} %get-tuple-element.9, bf16[1,16,8,32,128]{4,1,3,2,0:T(8,128)(2,1)S(1)} %get-tuple-element.8), kind=kLoop, calls=%fused_computation.31 | loop fusion | flops 32531200 | bytes 5450240 | tf_op jit(solution)/shard_map/concatenate | solution.py:16
  269.0 2.1 fusion.88
  275.0 2.2 fusion.85
  277.2 2.7 fusion.84
  281.7 2.1 fusion.81
  289.9 2.1 fusion.77
  293.9 2.2 fusion.75
  305.6 2.5 fusion.70
  308.1 2.1 fusion.69
  319.9 2.2 fusion.62
  323.9 21.7 %fusion.2 = f32[8,32,128,16,1]{2,3,0,1,4:T(8,128)} fusion(bf16[32,27,16,1,1]{0,2,3,4,1:T(8,128)(2,1)S(1)} %bitcast.525, bf16[1,27,32,8,32,128]{5,2,4,3,1,0:T(8,128)(2,1)} %fusion.61), kind=kOutput, calls=%fused_computation.2 | convolution fusion | flops 905969664 | bytes 58747904 | tf_op jit(solution)/shard_map/otc,etozhw->eczhw/dot_general | solution.py:59
  345.6 4.3 multiply_convert_fusion.1
  349.9 57.4 %fusion.106 = f32[1,1,32,432]{3,2,1,0:T(8,128)S(1)} fusion(bf16[432,8,32,128]{3,2,1,0:T(8,128)(2,1)} %bitcast.144, bf16[16,8,32,128]{3,0,2,1:T(8,128)(2,1)S(1)} %bitcast.518, bf16[16,8,32,128]{3,0,2,1:T(8,128)(2,1)S(1)} %bitcast.516), kind=kOutput, calls=%fused_computation.192 | convolution fusion | flops 910163968 | bytes 30464000 | tf_op jit(solution)/shard_map/eozhw,ekzhw->eok/dot_general | solution.py:55
  409.1 105.2 %all-reduce.7.cloned.1.call-done = f32[1,27648]{1,0:T(1,128)} async-done(((f32[1,27648]{1,0:T(1,128)}), f32[1,27648]{1,0:T(1,128)}) %all-reduce.7.cloned.1.call-update) | async-done | bytes 110608 | tf_op jit(solution)/shard_map/psum | solution.py:105
  519.1 3.4 collective-permute-start.6
  523.8 12.2 %all-reduce.9.cloned.1.call-done = f32[27648]{0:T(1024)} async-done(((f32[27648]{0:T(1024)}), f32[27648]{0:T(1024)}) %all-reduce.9.cloned.1.call-update) | async-done | bytes 110608 | tf_op jit(solution)/shard_map/psum | solution.py:109
  537.7 6.8 %select_maximum_fusion = bf16[1,32,10,34,130]{4,1,3,2,0:T(8,128)(2,1)S(1)} fusion(bf16[1,32,1,32,128]{4,1,3,2,0:T(8,128)(2,1)} %collective-permute-done.7, bf16[1,32,1,32,128]{4,1,3,2,0:T(8,128)(2,1)S(1)} %collective-permute-done.6, bf16[1,16,8,32,128]{4,1,3,2,0:T(8,128)(2,1)S(1)} %get-tuple-element.7, bf16[1,16,8,32,128]{4,1,3,2,0:T(8,128)(2,1)S(1)} %get-tuple-element.6), kind=kLoop, calls=%fused_computation.28 | loop fusion | flops 32531200 | bytes 5450240 | tf_op jit(solution)/shard_map/concatenate | solution.py:16
  544.4 2.1 fusion.60
  550.5 2.2 fusion.57
  552.6 2.7 fusion.56
  565.3 2.1 fusion.49
  569.3 2.2 fusion.47
  581.1 2.3 fusion.42
  583.4 2.1 fusion.41
  595.1 2.2 fusion.34
  599.1 21.9 %fusion = f32[8,32,128,16,1]{2,3,0,1,4:T(8,128)} fusion(bf16[32,27,16,1,1]{0,2,3,4,1:T(8,128)(2,1)S(1)} %bitcast.526, bf16[1,27,32,8,32,128]{5,2,4,3,1,0:T(8,128)(2,1)} %fusion.33), kind=kOutput, calls=%fused_computation | convolution fusion | flops 905969664 | bytes 58747904 | tf_op jit(solution)/shard_map/otc,etozhw->eczhw/dot_general | solution.py:59
  621.1 2.4 bitcast_add_fusion
  (132 shorter events, 155.3 us)
Async XLA Ops:
  7.2 507.1 %all-reduce.7.cloned.1.call-start = ((), (), s32[]{:S(2)}) async-start(), calls=%async_computation | async-start | bytes 221184 | tf_op jit(solution)/shard_map/psum | solution.py:105
  8.2 7.6 %collective-permute-start = (bf16[1,16,1,32,128]{4,3,2,1,0:T(8,128)(2,1)S(1)}, bf16[1,16,1,32,128]{4,3,2,1,0:T(8,128)(2,1)S(1)}, u32[]{:S(2)}, u32[]{:S(2)}) collective-permute-start(bf16[1,16,1,32,128]{4,3,2,1,0:T(8,128)(2,1)S(1)} %get-tuple-element.16), channel_id=1, source_target_pairs={{0,1},{1,2},{2,3},{3,4},{4,5},{5,6},{6,7},{7,8},{8,9},{9,10},{10,1... | collective-permute-start | bytes 393224 | tf_op jit(solution)/shard_map/ppermute | solution.py:14
  13.1 7.5 %collective-permute-start.1 = (bf16[1,16,1,32,128]{4,3,2,1,0:T(8,128)(2,1)S(1)}, bf16[1,16,1,32,128]{4,3,2,1,0:T(8,128)(2,1)S(1)}, u32[]{:S(2)}, u32[]{:S(2)}) collective-permute-start(bf16[1,16,1,32,128]{4,3,2,1,0:T(8,128)(2,1)S(1)} %get-tuple-element.17), channel_id=1, source_target_pairs={{1,0},{2,1},{3,2},{4,3},{5,4},{6,5},{7,6},{8,7},{9,8},{10,9},{11,1... | collective-permute-start | bytes 393224 | tf_op jit(solution)/shard_map/ppermute | solution.py:15
  15.4 14.7 %copy-start.1 = (bf16[1,16,8,32,128]{4,3,2,1,0:T(8,128)(2,1)S(1)}, bf16[1,16,8,32,128]{4,3,2,1,0:T(8,128)(2,1)}, u32[]{:S(2)}) copy-start(bf16[1,16,8,32,128]{4,3,2,1,0:T(8,128)(2,1)} %param.6) | copy-start | bytes 3145732
  69.8 26.2 %copy-start.4 = (bf16[2,32,432]{2,1,0:T(8,128)(2,1)S(1)}, bf16[2,32,432]{2,1,0:T(8,128)(2,1)}, u32[]{:S(2)}) copy-start(bf16[2,32,432]{2,1,0:T(8,128)(2,1)} %param.11) | copy-start | bytes 165892
  107.6 2.1 copy-start
  110.9 7.7 %collective-permute-start.2 = (bf16[1,16,1,32,128]{4,1,3,2,0:T(8,128)(2,1)S(1)}, bf16[1,16,1,32,128]{4,1,3,2,0:T(8,128)(2,1)S(1)}, u32[]{:S(2)}, u32[]{:S(2)}) collective-permute-start(bf16[1,16,1,32,128]{4,1,3,2,0:T(8,128)(2,1)S(1)} %get-tuple-element.14), channel_id=1, source_target_pairs={{0,1},{1,2},{2,3},{3,4},{4,5},{5,6},{6,7},{7,8},{8,9},{9,10},{10,1... | collective-permute-start | bytes 393224 | tf_op jit(solution)/shard_map/ppermute | solution.py:14
  114.5 6.9 %collective-permute-start.3 = (bf16[1,16,1,32,128]{4,1,3,2,0:T(8,128)(2,1)S(1)}, bf16[1,16,1,32,128]{4,1,3,2,0:T(8,128)(2,1)S(1)}, u32[]{:S(2)}, u32[]{:S(2)}) collective-permute-start(bf16[1,16,1,32,128]{4,1,3,2,0:T(8,128)(2,1)S(1)} %get-tuple-element.15), channel_id=1, source_target_pairs={{1,0},{2,1},{3,2},{4,3},{5,4},{6,5},{7,6},{8,7},{9,8},{10,9},{11,1... | collective-permute-start | bytes 393224 | tf_op jit(solution)/shard_map/ppermute | solution.py:15
  177.9 28.2 %copy-start.2 = (bf16[1,16,8,32,128]{4,3,2,1,0:T(8,128)(2,1)S(1)}, bf16[1,16,8,32,128]{4,3,2,1,0:T(8,128)(2,1)}, u32[]{:S(2)}) copy-start(bf16[1,16,8,32,128]{4,3,2,1,0:T(8,128)(2,1)} %param.7) | copy-start | bytes 3145732
  208.3 53.9 %collective-permute-start.4 = (bf16[1,32,1,32,128]{4,1,3,2,0:T(8,128)(2,1)}, bf16[1,32,1,32,128]{4,1,3,2,0:T(8,128)(2,1)S(1)}, u32[]{:S(2)}, u32[]{:S(2)}) collective-permute-start(bf16[1,32,1,32,128]{4,1,3,2,0:T(8,128)(2,1)} %get-tuple-element.12), channel_id=1, source_target_pairs={{0,1},{1,2},{2,3},{3,4},{4,5},{5,6},{6,7},{7,8},{8,9},{9,10},{10,1... | collective-permute-start | bytes 786440 | tf_op jit(solution)/shard_map/ppermute | solution.py:14
  212.3 49.9 %collective-permute-start.5 = (bf16[1,32,1,32,128]{4,1,3,2,0:T(8,128)(2,1)}, bf16[1,32,1,32,128]{4,1,3,2,0:T(8,128)(2,1)}, u32[]{:S(2)}, u32[]{:S(2)}) collective-permute-start(bf16[1,32,1,32,128]{4,1,3,2,0:T(8,128)(2,1)} %get-tuple-element.13), channel_id=1, source_target_pairs={{1,0},{2,1},{3,2},{4,3},{5,4},{6,5},{7,6},{8,7},{9,8},{10,9},{11,1... | collective-permute-start | bytes 786440 | tf_op jit(solution)/shard_map/ppermute | solution.py:15
  317.8 6.1 copy-start.6
  349.9 57.4 %copy-start.8 = (f32[1,1,32,432]{3,2,1,0:T(8,128)S(1)}, f32[1,1,32,432]{3,2,1,0:T(8,128)}, u32[]{:S(2)}) copy-start(f32[1,1,32,432]{3,2,1,0:T(8,128)} %fusion.101) | copy-start | bytes 165892
  349.9 58.4 %copy-start.5 = (bf16[1,32,432]{2,1,0:T(8,128)(2,1)S(1)}, bf16[1,32,432]{2,1,0:T(8,128)(2,1)}, u32[]{:S(2)}) copy-start(bf16[1,32,432]{2,1,0:T(8,128)(2,1)} %get-tuple-element.21) | copy-start | bytes 82948
  408.2 127.7 %all-reduce.9.cloned.1.call-start = ((), (), s32[]{:S(2)}) async-start(), calls=%async_computation.1 | async-start | bytes 221184 | tf_op jit(solution)/shard_map/psum | solution.py:109
  519.1 18.5 %collective-permute-start.6 = (bf16[1,32,1,32,128]{4,1,3,2,0:T(8,128)(2,1)}, bf16[1,32,1,32,128]{4,1,3,2,0:T(8,128)(2,1)S(1)}, u32[]{:S(2)}, u32[]{:S(2)}) collective-permute-start(bf16[1,32,1,32,128]{4,1,3,2,0:T(8,128)(2,1)} %get-tuple-element.10), channel_id=1, source_target_pairs={{0,1},{1,2},{2,3},{3,4},{4,5},{5,6},{6,7},{7,8},{8,9},{9,10},{10,1... | collective-permute-start | bytes 786440 | tf_op jit(solution)/shard_map/ppermute | solution.py:14
  522.5 15.2 %collective-permute-start.7 = (bf16[1,32,1,32,128]{4,1,3,2,0:T(8,128)(2,1)}, bf16[1,32,1,32,128]{4,1,3,2,0:T(8,128)(2,1)}, u32[]{:S(2)}, u32[]{:S(2)}) collective-permute-start(bf16[1,32,1,32,128]{4,1,3,2,0:T(8,128)(2,1)} %get-tuple-element.11), channel_id=1, source_target_pairs={{1,0},{2,1},{3,2},{4,3},{5,4},{6,5},{7,6},{8,7},{9,8},{10,9},{11,1... | collective-permute-start | bytes 786440 | tf_op jit(solution)/shard_map/ppermute | solution.py:15
  593.1 6.1 copy-start.7
  599.1 21.9 %copy-start.3 = (f32[8,32,128,16,1]{2,3,0,1,4:T(8,128)S(1)}, f32[8,32,128,16,1]{2,3,0,1,4:T(8,128)}, u32[]{:S(2)}) copy-start(f32[8,32,128,16,1]{2,3,0,1,4:T(8,128)} %fusion.2) | copy-start | bytes 6291460
Sparse Core Ops, SparseCore 0:
  408.3 105.8 all-reduce.6
  518.4 17.5 all-reduce.8
where the time goes:
time: 643 us; the launch traced here: 633 us
  local copies, waits for them, and re-layouts  227 us (35%)
  matrix products  189 us (29%)
  waiting for transfers between devices  125 us (19%)
  other arithmetic  52.5 us (8%)
  starting transfers between devices  21.1 us (3%)
  between operations  16.7 us (3%)
    unnamed x113, local copies, waits for them, and re-layouts  170 us
    dot_general x2, matrix products, layer_backward(): jnp.einsum('eozhw,ekzhw->eok', delta, patches, preferred_element_type=jnp...  106 us
    psum x1, waiting for transfers between devices, per_device(): summed = lax.psum(flat, 'slab')  105 us
    another operation x4, local copies, waits for them, and re-layouts, columns(): stacked = jnp.stack(taps, axis=1)  49.3 us
    dot_general x2, matrix products, layer_backward(): jnp.einsum('otc,etozhw->eczhw', shaped, back_columns(extended), preferred...  43.7 us
    dot_general x2, matrix products, layer_forward(): jnp.einsum('ok,ekzhw->eozhw', kernel, patches, preferred_element_type=jnp...  39.9 us
    concatenate x4, other arithmetic, with_halo(): array = jnp.concatenate([before, array, after], axis=dim)  19.5 us
    unnamed x10, other arithmetic  16.9 us
  transfers between devices with their start and end apart: 10, of which 5 were waited for; matrix products, arithmetic and copies ran while one was open for 9% of the time, Pallas kernels for 0%

commit v1 on v0

v1 whole, which is shorter than its diff:
```python
import functools
import jax
import jax.numpy as jnp
from jax import lax
from jax.experimental import pallas as pl
from jax.experimental.pallas import tpu as pltpu
from jax.sharding import PartitionSpec as P

F32, BF16 = jnp.float32, jnp.bfloat16
PZ, PH = 2, 4
WZ, WH = PZ + 2, PH + 2
VMEM = pltpu.VMEM


def with_halo(array, sides, width):
    for axis, dim in sides:
        peers, length = (lax.axis_size(axis), array.shape[dim])
        up = [(i, (i + 1) % peers) for i in range(peers - 1)]
        down = [(j, i) for i, j in up]
        last = lax.slice_in_dim(array, length - width, length, axis=dim)
        leading = lax.slice_in_dim(array, 0, width, axis=dim)
        before = lax.ppermute(last, axis, up)
        after = lax.ppermute(leading, axis, down)
        array = jnp.concatenate([before, array, after], axis=dim)
    return array


def shifted_stack(extended, flip):
    zs = extended.shape[2] - 2
    hs, ws = (extended.shape[3], extended.shape[4])
    padded = jnp.pad(extended, ((0, 0), (0, 0), (0, 0), (1, 1), (1, 1)))
    taps = []
    for tap in range(27):
        dz, dh, dw = tap // 9, tap // 3 % 3, tap % 3
        if flip:
            dz, dh, dw = 2 - dz, 2 - dh, 2 - dw
        taps.append(padded[:, :, dz : dz + zs, dh : dh + hs, dw : dw + ws])
    return jnp.stack(taps, axis=1)


def layer_forward(field, kernel):
    patches = shifted_stack(with_halo(field, (("slab", 2),), 1), False)
    ex, taps, chans, zs, hs, ws = patches.shape
    patches = patches.reshape((ex, taps * chans, zs, hs, ws))
    pre = jnp.einsum("ok,ekzhw->eozhw", kernel, patches, preferred_element_type=F32)
    return (pre, patches)


def layer_backward(delta, kernel, patches):
    grads = jnp.einsum("eozhw,ekzhw->eok", delta, patches, preferred_element_type=F32)
    extended = with_halo(delta, (("slab", 2),), 1)
    shaped = kernel.reshape((kernel.shape[0], 27, kernel.shape[1] // 27))
    spread = jnp.einsum(
        "otc,etozhw->eczhw", shaped, shifted_stack(extended, True), preferred_element_type=F32
    )
    return (grads, spread)


def plain_device(volume, cotangent, gate_mask, loss_scale, canary, kernels):
    chans = volume.shape[1]
    local_ex = volume.shape[0]
    mask_one = gate_mask[:, 0][:, None].astype(F32)
    mask_two = gate_mask[:, 1][:, None].astype(F32)
    pre_one, patches_one = layer_forward(volume, kernels[0])
    value_one = pre_one[:, :chans]
    sig_one = jax.nn.sigmoid(pre_one[:, chans:])
    hidden = (volume.astype(F32) + value_one * sig_one * mask_one).astype(BF16)
    pre_two, patches_two = layer_forward(hidden, kernels[1])
    value_two = pre_two[:, :chans]
    sig_two = jax.nn.sigmoid(pre_two[:, chans:])
    weights = channel_weights(chans, loss_scale, canary)
    grad_out = cotangent.astype(F32) * weights[:, :, None, None, None]
    delta_two = jnp.concatenate(
        [
            grad_out * sig_two * mask_two,
            grad_out * value_two * sig_two * (1.0 - sig_two) * mask_two,
        ],
        axis=1,
    ).astype(BF16)
    grad_two, spread_two = layer_backward(delta_two, kernels[1], patches_two)
    grad_hidden = grad_out + spread_two
    delta_one = jnp.concatenate(
        [
            grad_hidden * sig_one * mask_one,
            grad_hidden * value_one * sig_one * (1.0 - sig_one) * mask_one,
        ],
        axis=1,
    ).astype(BF16)
    grad_one, spread_one = layer_backward(delta_one, kernels[0], patches_one)
    input_grad = grad_hidden + spread_one
    flat = jnp.stack([grad_one, grad_two], axis=1).reshape((local_ex, -1))
    bound, scaling = clip_numbers(volume, kernels)
    summed = lax.psum(flat, "slab")
    norm = jnp.sqrt(jnp.sum(summed * summed, axis=1) + 1e-06)
    factor = jnp.minimum(1.0, bound / norm)
    total = lax.psum(jnp.sum(summed * factor[:, None], axis=0), "ex")
    return (input_grad, (total * scaling).reshape(kernels.shape))


def channel_weights(chans, loss_scale, canary):
    ids = jnp.arange(chans, dtype=jnp.int32)
    return (1.0 + 2.0 * (ids[None, :] == canary[:, None]).astype(F32)) * loss_scale[:, None]


def clip_numbers(volume, kernels):
    chans = volume.shape[1]
    depth = volume.shape[2] * lax.axis_size("slab")
    bound = 20.0 * jnp.sqrt(F32(depth * volume.shape[3] * volume.shape[4]))
    examples = volume.shape[0] * lax.axis_size("ex")
    scaling = jnp.sqrt(F32(108 * chans * chans)) / (bound * jnp.sqrt(F32(examples)))
    return bound, scaling


def side_shifts(tile):
    lane = lax.broadcasted_iota(jnp.int32, tile.shape, tile.ndim - 1)
    last = tile.shape[-1] - 1
    before = jnp.where(lane == 0, 0.0, pltpu.roll(tile, 1, tile.ndim - 1))
    after = jnp.where(lane == last, 0.0, pltpu.roll(tile, last, tile.ndim - 1))
    return before, after


def put_rows(ref, plane, h, tile):
    rows, chans = tile.shape[:2]
    before, after = side_shifts(tile)
    for s, part in enumerate((before, tile, after)):
        ref[plane, pl.ds(h + 1, rows), s * chans : (s + 1) * chans, :] = part.astype(BF16)


def put_pair_rows(ref, plane, h, top, low):
    rows, chans = top.shape[:2]
    for first, tile in ((0, top), (chans, low)):
        before, after = side_shifts(tile)
        for s, part in enumerate((before, tile, after)):
            at = s * 2 * chans + first
            ref[plane, pl.ds(h + 1, rows), at : at + chans, :] = part.astype(BF16)


def clear_edges(ref):
    for plane in range(ref.shape[0]):
        zero = jnp.zeros(ref.shape[2:], BF16)
        ref[plane, 0] = zero
        ref[plane, ref.shape[1] - 1] = zero


def windows(planes, blocks):
    cols = []
    for h in blocks:
        parts = []
        for ref, at in planes:
            part = ref[at, pl.ds(h, WH)]
            parts.append(part.reshape((-1, part.shape[-1])))
        cols.append(jnp.concatenate(parts, axis=0))
    return jnp.concatenate(cols, axis=1)


def conv_blocks(mat, planes, h):
    out = jnp.dot(mat, windows(planes, (h, h + PH)), preferred_element_type=F32)
    return out.reshape((PZ * PH, -1, out.shape[-1]))


def split_blocks(tile, fn):
    half = tile.shape[-1] // 2
    for pz in range(PZ):
        for b in range(2):
            fn(pz, b, tile[pz * PH : (pz + 1) * PH, :, b * half : (b + 1) * half])


def join_blocks(fn):
    return jnp.concatenate(
        [jnp.concatenate([fn(pz, 0), fn(pz, 1)], axis=2) for pz in range(PZ)], axis=0
    )


def mask_blocks(mask_planes, h, chans):
    parts = []
    for pz in range(PZ):
        ref, at = mask_planes[pz]
        rows = ref[at + (pl.ds(h, 2 * PH),)].astype(F32)
        both = jnp.concatenate([rows[:PH], rows[PH:]], axis=1)
        parts.append(jnp.broadcast_to(both[:, None, :], (PH, chans, both.shape[1])))
    return jnp.concatenate(parts, axis=0)


def row_loop(hs, body):
    def step(i, carry):
        body(pl.multiple_of(i * (2 * PH), 2 * PH))
        return carry

    lax.fori_loop(0, hs // (2 * PH), step, 0)


def forward_one(mat_ref, v_planes, v_centre, mask_planes, x1, x1_at, gates, gates_at, hs, chans):
    def body(h):
        pre = conv_blocks(mat_ref[...], v_planes, h)
        val, sig = pre[:, :chans], jax.nn.sigmoid(pre[:, chans:])
        mask = mask_blocks(mask_planes, h, chans)

        def centre(pz, b):
            ref, at = v_centre[pz]
            return ref[at, pl.ds(h + b * PH + 1, PH), chans : 2 * chans, :].astype(F32)

        open_ = sig * mask
        hid = join_blocks(centre) + val * open_
        slope = val * open_ * (1.0 - sig)
        split_blocks(hid, lambda pz, b, t: put_rows(x1, x1_at + pz, h + b * PH, t))

        def keep(which):
            def put(pz, b, t):
                gates[which, gates_at + pz, pl.ds(h + b * PH, PH)] = t

            return put

        split_blocks(open_, keep(0))
        split_blocks(slope, keep(1))

    row_loop(hs, body)


def forward_two(mat_ref, x1_planes, mask_planes, dy_fn, d2, d2_at, hs, chans):
    def body(h):
        pre = conv_blocks(mat_ref[...], x1_planes, h)
        val, sig = pre[:, :chans], jax.nn.sigmoid(pre[:, chans:])
        dy = join_blocks(lambda pz, b: dy_fn(pz, h + b * PH))
        top = dy * sig * mask_blocks(mask_planes, h, chans)
        low = top * val * (1.0 - sig)
        half = top.shape[-1] // 2
        for pz in range(PZ):
            for b in range(2):
                at = (slice(pz * PH, (pz + 1) * PH), slice(None), slice(b * half, (b + 1) * half))
                put_pair_rows(d2, d2_at + pz, h + b * PH, top[at], low[at])

    row_loop(hs, body)


def backward_two(mat, d2_planes, dy_fn, gates, gates_at, dx, dx_at, d1, d1_at, hs):
    def body(h):
        spread = conv_blocks(mat(), d2_planes, h)
        half = spread.shape[-1] // 2
        for pz in range(PZ):
            for b in range(2):
                row = h + b * PH
                part = spread[pz * PH : (pz + 1) * PH, :, b * half : (b + 1) * half]
                if dy_fn[pz] is not None:
                    part = part + dy_fn[pz](row)
                dx[dx_at + pz, pl.ds(row, PH)] = part
                put_pair_rows(
                    d1,
                    d1_at + pz,
                    row,
                    part * gates[0, gates_at + pz, pl.ds(row, PH)],
                    part * gates[1, gates_at + pz, pl.ds(row, PH)],
                )

    row_loop(hs, body)


def weight_blocks(x_planes, d_planes, acc, hs):
    blocks = tuple(range(0, hs, PH))
    lhs = windows(x_planes, blocks)
    cols = []
    for h in blocks:
        parts = []
        for ref, at in d_planes:
            outs = ref.shape[2] // 3
            parts.append(ref[at, h + 1 : h + 1 + PH, outs : 2 * outs, :].reshape((PH * outs, -1)))
        cols.append(jnp.concatenate(parts, axis=0))
    rhs = jnp.concatenate(cols, axis=1)
    acc[...] += lax.dot_general(lhs, rhs, (((1,), (1,)), ((), ())), preferred_element_type=F32)


def fold_blocks(acc, outs, chans):
    taps = 9 * chans
    width = PH * outs
    rows = WH * 3 * chans
    total = None
    for ph in range(PH):
        part = None
        for pz in range(PZ):
            pieces = []
            for dz in range(3):
                at = (pz + dz) * rows + ph * 3 * chans
                pieces.append(acc[at : at + taps, pz * width : (pz + 1) * width])
            piece = jnp.concatenate(pieces, axis=0)
            part = piece if part is None else part + piece
        if ph:
            part = pltpu.roll(part, width - ph * outs, 1)
        total = part if total is None else total + part
    return total


def place_matrix(cols, stride, total, piece):
    k = lax.broadcasted_iota(jnp.int32, (cols, total), 0)
    j = lax.broadcasted_iota(jnp.int32, (cols, total), 1)
    group = (k >= piece).astype(jnp.int32) + (k >= 2 * piece).astype(jnp.int32)
    return (j == k + group * (stride - piece)).astype(F32).astype(BF16)


def spread_kernel(rows, out_ref, layer, width):
    outs, cols = rows.shape
    stride = WH * width
    place = place_matrix(cols, stride, WZ * stride, 3 * width)
    base = jnp.dot(rows, place, preferred_element_type=F32)
    for pz in range(PZ):
        for ph in range(PH):
            at = (pz * PH + ph) * outs
            shift = pz * stride + ph * width
            tile = pltpu.roll(base, shift, 1) if shift else base
            out_ref[layer, at : at + outs, :] = tile.astype(BF16)


def to_rows(source, scratch, put):
    chans, hs, ws = source.shape
    scratch[...] = source.astype(F32).reshape((chans * hs, ws))
    for h in range(hs):
        put(h, scratch[pl.ds(h, chans, stride=hs), :])


def inner_kernel(zs, vol, cot, mask, wts, ker, kft, mf, mb, xv, ct, x1, g1, d2, dx, d1, t1, t2, rows):
    chans, hs = vol.shape[0], vol.shape[2]
    for layer in range(2):
        spread_kernel(ker[layer], mf, layer, 3 * chans)
        spread_kernel(kft[layer], mb, layer, 6 * chans)
    for ref in (xv, x1, d2, d1):
        clear_edges(ref)

    def arrange(z, carry):
        to_rows(vol[:, z], rows, lambda h, t: put_rows(xv, z, h, t[None]))

        def put(h, t):
            ct[z, h] = (t * wts[...]).astype(F32)

        to_rows(cot[:, z], rows, put)
        return carry

    lax.fori_loop(0, zs, arrange, 0)

    def layer_one(k, carry):
        z = 2 * k + 1
        forward_one(
            mf.at[0],
            [(xv, z - 1 + i) for i in range(WZ)],
            [(xv, z + i) for i in range(PZ)],
            [(mask, (0, z + i)) for i in range(PZ)],
            x1, 2 * k, g1, 2 * k, hs, chans,
        )
        return carry

    lax.fori_loop(0, (zs - 2) // 2, layer_one, 0)
    t1[...] = jnp.zeros_like(t1)
    t2[...] = jnp.zeros_like(t2)

    def layer_two(k, carry):
        z = 2 * k + 2
        x_planes = [(x1, z - 2 + i) for i in range(WZ)]
        forward_two(
            mf.at[1], x_planes, [(mask, (1, z + i)) for i in range(PZ)],
            lambda pz, h: ct[z + pz, pl.ds(h, PH)], d2, 2 * k, hs, chans,
        )
        weight_blocks(x_planes, [(d2, 2 * k + i) for i in range(PZ)], t2, hs)
        return carry

    lax.fori_loop(0, (zs - 4) // 2, layer_two, 0)

    def layer_back(k, carry):
        z = 2 * k + 3
        dys = [lambda h, i=i: ct[z + i, pl.ds(h, PH)] for i in range(PZ)]
        backward_two(
            lambda: mb[1], [(d2, z - 3 + i) for i in range(WZ)], dys, g1, z - 1, dx, 2 * k, d1, 2 * k, hs
        )
        weight_blocks(
            [(xv, z - 1 + i) for i in range(WZ)], [(d1, 2 * k + i) for i in range(PZ)], t1, hs
        )
        return carry

    lax.fori_loop(0, (zs - 6) // 2, layer_back, 0)


def edge_kernel(low, halo, xv, x1, d2, gates, mask, ct, mf, mb,
                send, dx, d1, t1, t2, xh, x1h, d2h, gh, rows):
    chans, hs = xv.shape[2] // 3, xv.shape[1] - 2
    for ref in (xh, x1h, d2h, d1):
        clear_edges(ref)
    for i in range(2):
        to_rows(halo[i * chans : (i + 1) * chans], rows, lambda h, t: put_rows(xh, i, h, t[None]))
    outer = (halo, (2 * chans,))
    if low:
        v_planes = [(xh, 0), (xh, 1), (xv, 0), (xv, 1)]
        v_centre = [(xh, 1), (xv, 0)]
        masks1 = [outer, (mask, (0, 0))]
        masks2 = [(mask, (1, 0)), (mask, (1, 1))]
        x_planes = [(x1h, 0), (x1h, 1), (x1, 0), (x1, 1)]
        d_edge = [(d2h, 0), (d2h, 1)]
        half = slice(mb.shape[2] // 2, mb.shape[2])
        dy_edge = [None, lambda h: ct[0, pl.ds(h, PH)]]
        d_next = [(d2h, 0), (d2h, 1), (d2, 0), (d2, 1)]
        dy_next = [lambda h, i=i: ct[1 + i, pl.ds(h, PH)] for i in range(2)]
        at_edge, at_next, base = 0, 2, 0
        dy_two = lambda pz, h: ct[pz, pl.ds(h, PH)]
        v_next = [(xv, i) for i in range(4)]
    else:
        v_planes = [(xv, 2), (xv, 3), (xh, 0), (xh, 1)]
        v_centre = [(xv, 3), (xh, 0)]
        masks1 = [(mask, (0, 3)), outer]
        masks2 = [(mask, (1, 2)), (mask, (1, 3))]
        x_planes = [(x1, 0), (x1, 1), (x1h, 0), (x1h, 1)]
        d_edge = [(d2h, 0), (d2h, 1)]
        half = slice(0, mb.shape[2] // 2)
        dy_edge = [lambda h: ct[3, pl.ds(h, PH)], None]
        d_next = [(d2, 0), (d2, 1), (d2h, 0), (d2h, 1)]
        dy_next = [lambda h, i=i: ct[1 + i, pl.ds(h, PH)] for i in range(2)]
        at_edge, at_next, base = 2, 0, 0
        dy_two = lambda pz, h: ct[2 + pz, pl.ds(h, PH)]
        v_next = [(xv, i) for i in range(4)]
    forward_one(mf.at[0], v_planes, v_centre, masks1, x1h, 0, gh, 0, hs, chans)
    forward_two(mf.at[1], x_planes, masks2, dy_two, d2h, 0, hs, chans)
    backward_two(lambda: mb[1, :, half], d_edge, dy_edge, gh, 0, dx, at_edge, d1, at_edge, hs)

    outside = 0 if low else 1

    def spread(h):
        out = conv_blocks(mb[0, :, half], [(d1, at_edge), (d1, at_edge + 1)], h)
        width = out.shape[-1] // 2
        for pz in range(PZ):
            for b in range(2):
                row = h + b * PH
                part = out[pz * PH : (pz + 1) * PH, :, b * width : (b + 1) * width]
                if pz == 1 - outside:
                    part = part + dx[at_edge + outside, pl.ds(row, PH)]
                send[pz, pl.ds(row, PH)] = part.astype(BF16)

    row_loop(hs, spread)
    t1[...] = jnp.zeros_like(t1)
    t2[...] = jnp.zeros_like(t2)
    weight_blocks(x_planes, [(d2h, 0), (d2h, 1)], t2, hs)
    weight_blocks(v_planes, [(d1, at_edge + i) for i in range(2)], t1, hs)
    backward_two(lambda: mb[1], d_next, dy_next, gates, 0, dx, at_next, d1, at_next, hs)
    weight_blocks(v_next, [(d1, at_next + i) for i in range(2)], t1, hs)


def fold_kernel(a1, a2, b1, b2, c1, c2, out, acc):
    chans = a1.shape[0] // (WZ * WH * 3)
    outs = 2 * chans
    acc[...] = a1[...] + b1[...] + c1[...]
    one = fold_blocks(acc, outs, chans)
    acc[...] = a2[...] + b2[...] + c2[...]
    two = fold_blocks(acc, outs, chans)
    lane = lax.broadcasted_iota(jnp.int32, one.shape, 1)
    both = jnp.where(lane < outs, one, pltpu.roll(two, outs, 1))
    half = both.shape[0] // 2
    lane = lax.broadcasted_iota(jnp.int32, (half, both.shape[1]), 1)
    out[...] = jnp.where(lane < 2 * outs, both[:half], pltpu.roll(both[half:], 2 * outs, 1))


def output_kernel(zs, mb, d1a, d1b, d1c, dxa, dxb, dxc, lo, hi, out, rows):
    chans, hs, ws = out.shape[0], out.shape[2], out.shape[3]

    def plane_of(refs, z):
        if z <= 2:
            return (refs[0], z + 1)
        if z <= zs - 4:
            return (refs[1], z - 3)
        return (refs[2], z - (zs - 3))

    for z in range(0, zs, 2):
        planes = [plane_of((d1a, d1b, d1c), z - 1 + i) for i in range(WZ)]
        dxs = [plane_of((dxa, dxb, dxc), z + i) for i in range(PZ)]
        extra = lo if z == 0 else hi if z == zs - 2 else None

        def body(h):
            res = conv_blocks(mb[0], planes, h)
            width = res.shape[-1] // 2
            for pz in range(PZ):
                for b in range(2):
                    row = h + b * PH
                    part = res[pz * PH : (pz + 1) * PH, :, b * width : (b + 1) * width]
                    ref, at = dxs[pz]
                    part = part + ref[at, pl.ds(row, PH)]
                    if extra is not None:
                        part = part + extra[pz, pl.ds(row, PH)].astype(F32)
                    at = pl.multiple_of(row * chans, chans)
                    rows[pz, pl.ds(at, PH * chans), :] = part.reshape((PH * chans, ws))

        row_loop(hs, body)
        for pz in range(PZ):
            for c in range(chans):
                out[c, z + pz] = rows[pz, pl.ds(c, hs, stride=chans), :]


def clip_kernel(mine, other, bound, scaling, out):
    total = None
    for ref in (mine, other):
        value = ref[...]
        norm = jnp.sqrt(jnp.sum(value * value, keepdims=True) + 1e-06)
        part = value * jnp.minimum(1.0, bound[...] / norm)
        total = part if total is None else total + part
    total = total * scaling[...]
    outs = out.shape[1]
    half = total.shape[0]
    flat = total.T
    for layer in range(2):
        for part in range(2):
            at = (part * 2 + layer) * outs
            out[layer, :, part * half : (part + 1) * half] = flat[at : at + outs]


def call(body, outs, scratch=(), flops=0, vmem=56 << 20):
    def run(*args):
        size = sum(a.size * a.dtype.itemsize for a in args) + sum(o.size * o.dtype.itemsize for o in outs)
        return pl.pallas_call(
            body,
            out_shape=outs,
            scratch_shapes=list(scratch),
            compiler_params=pltpu.CompilerParams(vmem_limit_bytes=vmem),
            cost_estimate=pl.CostEstimate(flops=flops, bytes_accessed=size, transcendentals=0),
        )(*args)

    return run


def shape(*dims, dtype=F32):
    return jax.ShapeDtypeStruct(dims, dtype)


def sum_over_slab(value):
    peers = lax.axis_size("slab")
    step = 1
    order = []
    while step < peers:
        order.append(step)
        step *= 2
    for step in order[1:] + order[:1]:
        value = value + lax.ppermute(value, "slab", [(i, i ^ step) for i in range(peers)])
    return value


def block_device(volume, cotangent, gate_mask, loss_scale, canary, kernels):
    chans, zs, hs, ws = volume.shape[1:]
    outs = 2 * chans
    vol, cot, mask = volume[0], cotangent[0], gate_mask[0]
    peers = lax.axis_size("slab")
    up = [(i, i + 1) for i in range(peers - 1)]
    down = [(i + 1, i) for i in range(peers - 1)]

    def packed(first, edge):
        planes = [vol[:, first], vol[:, first + 1], mask[0, edge][None].astype(BF16)]
        return jnp.concatenate(planes, axis=0)

    below = lax.ppermute(packed(zs - 2, zs - 1), "slab", up)
    above = lax.ppermute(packed(0, 0), "slab", down)

    wts = jnp.broadcast_to(channel_weights(chans, loss_scale, canary)[0][:, None], (chans, ws))
    kft = kernels.reshape((2, outs, 27, chans))[:, :, ::-1].transpose((0, 3, 2, 1))
    kft = kft.reshape((2, chans, 27 * outs))

    k_fwd, k_bwd = WZ * WH * 3 * chans, WZ * WH * 3 * outs
    m_fwd, m_bwd = PZ * PH * outs, PZ * PH * chans
    x_plane, d_plane, c_plane = (hs + 2, 3 * chans, ws), (hs + 2, 3 * outs, ws), (hs, chans, ws)
    acc = shape(k_fwd, m_fwd)
    rows = VMEM((chans * hs, ws), F32)
    pair = 2 * k_fwd * m_fwd * hs // PH * ws

    mf, mb, xv, ct, x1, g1, d2, dx_in, d1_in, t1_in, t2_in = call(
        functools.partial(inner_kernel, zs),
        [
            shape(2, m_fwd, k_fwd, dtype=BF16),
            shape(2, m_bwd, k_bwd, dtype=BF16),
            shape(zs, *x_plane, dtype=BF16),
            shape(zs, *c_plane),
            shape(zs - 2, *x_plane, dtype=BF16),
            shape(2, zs - 2, *c_plane),
            shape(zs - 4, *d_plane, dtype=BF16),
            shape(zs - 6, *c_plane),
            shape(zs - 6, *d_plane, dtype=BF16),
            acc,
            acc,
        ],
        [rows],
        flops=pair * 10,
    )(vol, cot, mask, wts, kernels, kft)

    def edge(low, halo):
        four = slice(0, 4) if low else slice(zs - 4, zs)
        two = slice(0, 2) if low else slice(zs - 4, zs - 2)
        two_d = slice(0, 2) if low else slice(zs - 6, zs - 4)
        return call(
            functools.partial(edge_kernel, low),
            [
                shape(2, *c_plane, dtype=BF16),
                shape(4, *c_plane),
                shape(4, *d_plane, dtype=BF16),
                acc,
                acc,
            ],
            [
                VMEM((2,) + x_plane, BF16),
                VMEM((2,) + x_plane, BF16),
                VMEM((2,) + d_plane, BF16),
                VMEM((2, 2) + c_plane, F32),
                rows,
            ],
            flops=pair * 8,
        )(halo, xv[four], x1[two], d2[two_d], g1[:, two], mask[:, four], ct[four], mf, mb)

    send_lo, dx_lo, d1_lo, t1_lo, t2_lo = edge(True, below)
    send_hi, dx_hi, d1_hi, t1_hi, t2_hi = edge(False, above)
    from_above = lax.ppermute(send_lo, "slab", down)
    from_below = lax.ppermute(send_hi, "slab", up)

    local = call_one(fold_kernel, shape(27 * chans // 2, 4 * outs), [VMEM((k_fwd, m_fwd), F32)])(
        t1_in, t2_in, t1_lo, t2_lo, t1_hi, t2_hi
    )
    mine = sum_over_slab(local)
    other = lax.ppermute(mine, "ex", [(0, 1), (1, 0)])
    first = lax.axis_index("ex") == 0
    bound, scaling = clip_numbers(volume, kernels)
    kernel_grad = call_one(clip_kernel, shape(*kernels.shape), [])(
        jnp.where(first, mine, other), jnp.where(first, other, mine),
        bound.reshape((1, 1)), scaling.reshape((1, 1)),
    )
    input_grad = call_one(
        functools.partial(output_kernel, zs), shape(chans, zs, hs, ws), [VMEM((2, chans * hs, ws), F32)],
        flops=pair * 4,
    )(mb, d1_lo, d1_in, d1_hi, dx_lo, dx_in, dx_hi, from_below, from_above)
    return (input_grad[None], kernel_grad)


def call_one(body, out, scratch, flops=0):
    run = call(body, [out], scratch, flops)
    return lambda *args: run(*args)[0]


def per_device(*args):
    ex, chans, zs, hs, ws = args[0].shape
    blocks = ex == 1 and lax.axis_size("ex") == 2 and chans == 16 and ws == 128
    blocks = blocks and hs % 16 == 0 and zs % 2 == 0 and zs >= 8
    peers = lax.axis_size("slab")
    if blocks and peers & (peers - 1) == 0:
        return block_device(*args)
    return plain_device(*args)


def solution(mesh):
    placed = (
        P("ex", None, "slab", None, None),
        P("ex", None, "slab", None, None),
        P("ex", None, "slab", None, None),
        P("ex"),
        P("ex"),
        P(),
    )
    return jax.shard_map(
        per_device,
        mesh=mesh,
        in_specs=placed,
        out_specs=(P("ex", None, "slab", None, None), P()),
        check_vma=False,
    )
```

time: 643 us -> 137 us (0.21); the launches traced: 633 us -> 137 us
  local copies, waits for them, and re-layouts: 227 us -> 19.7 us
  matrix products: 189 us -> 0 us
  waiting for transfers between devices: 125 us -> 16.4 us
  Pallas kernels: 0 us -> 75.1 us
  other arithmetic: 52.5 us -> 1.77 us
  between operations: 16.7 us -> 2.16 us
    dot_general x6 -> x0, matrix products: 189 us -> none  [the longest x2 106 us: layer_backward(): jnp.einsum('eozhw,ekzhw->eok', delta, patches, preferred_element_type=jnp...]
    unnamed x113 -> x26, local copies, waits for them, and re-layouts: 170 us -> 5.89 us
    psum x2 -> x0, waiting for transfers between devices: 117 us -> none  [the longest x1 105 us: per_device(): summed = lax.psum(flat, 'slab')]
    pallas_call x0 -> x6, Pallas kernels: none -> 75.1 us  [run(): pl.pallas_call(body, out_shape=outs, scratch_shapes=list(scratch), compil...]
    another operation x6 -> x0, local copies, waits for them, and re-layouts: 52.9 us -> none  [the longest x4 49.3 us: columns(): stacked = jnp.stack(taps, axis=1)]
    concatenate x4 -> x2, other arithmetic: 19.5 us -> 0.08 us  [packed(): return jnp.concatenate(planes, axis=0)]
    unnamed x10 -> x0, other arithmetic: 16.9 us -> none
    slice x5 -> x6, local copies, waits for them, and re-layouts: 3.17 us -> 12.1 us  [the longest x1 4.52 us: edge(): d2[two_d]]
  transfers between devices with their start and end apart: 10 -> 9, of which waited for: 5 -> 3; matrix products, arithmetic and copies ran while one was open for 9% -> 10% of each run, Pallas kernels for 0% -> 39%
where the time goes in v1:
time: 137 us
  Pallas kernels  75.1 us (55%)
  starting transfers between devices  21.7 us (16%)
  local copies, waits for them, and re-layouts  19.7 us (14%)
  waiting for transfers between devices  16.4 us (12%)
  between operations  2.16 us (2%)
  other arithmetic  1.77 us (1%)
    pallas_call x6, Pallas kernels, run(): pl.pallas_call(body, out_shape=outs, scratch_shapes=list(scratch), compil...  75.1 us
    ppermute x4, waiting for transfers between devices, sum_over_slab(): lax.ppermute(value, 'slab', [(i, i ^ step) for i in range(peers)])  16.4 us
    ppermute x4, starting transfers between devices, sum_over_slab(): lax.ppermute(value, 'slab', [(i, i ^ step) for i in range(peers)])  9.18 us
    unnamed x26, local copies, waits for them, and re-layouts  5.89 us
    ppermute x1, starting transfers between devices, block_device(): below = lax.ppermute(packed(zs - 2, zs - 1), 'slab', up)  5.49 us
    slice x1, local copies, waits for them, and re-layouts, edge(): d2[two_d]  4.52 us
    ppermute x1, starting transfers between devices, block_device(): from_below = lax.ppermute(send_hi, 'slab', up)  4.37 us
  transfers between devices with their start and end apart: 9, of which 3 were waited for; matrix products, arithmetic and copies ran while one was open for 10% of the time, Pallas kernels for 39%

profile of v1, /device:TPU:0, one launch (start us, length us, event | category | flops | bytes accessed | tf_op | source)
XLA Modules:
  0.0 136.8 jit_solution(9272441689926704082)
XLA Ops:
  0.6 0.0 copy-start.4
  0.6 1.4 copy.17
  2.0 0.0 copy-start.7
  2.1 0.0 copy-done.4
  2.2 1.3 collective-permute-start.1
  3.5 5.5 %collective-permute-start = (bf16[33,32,128]{2,1,0:T(8,128)(2,1)S(1)}, bf16[33,32,128]{2,1,0:T(8,128)(2,1)S(1)}, u32[]{:S(2)}, u32[]{:S(2)}) collective-permute-start(bf16[33,32,128]{2,1,0:T(8,128)(2,1)S(1)} %pad_maximum_fusion), channel_id=1, source_target_pairs={{0,1},{1,2},{2,3},{3,4},{4,5},{5,6},{6,7},{7,8},{8,9},{9,10},{10,1... | collective-permute-start | bytes 811016 | tf_op jit(solution)/shard_map/ppermute | solution.py:548
  9.0 0.2 copy.12
  9.2 0.1 copy.13
  9.3 0.9 reshape.55.kft
  11.5 0.7 fusion.7
  12.2 0.7 broadcast_in_dim.4.wts
  12.8 24.8 %shard_map.77 = (bf16[2,256,1152]{2,1,0:T(8,128)(2,1)}, bf16[2,128,2304]{2,1,0:T(8,128)(2,1)}, bf16[8,34,48,128]{3,2,1,0:T(8,128)(2,1)}, f32[8,32,16,128]{3,2,1,...) custom-call(bf16[16,8,32,128]{3,2,1,0:T(8,128)(2,1)} %bitcast.29, ...), custom_call_target="tpu_custom_call" | custom-call | flops 6039797760 | bytes 23826432 | tf_op jit(solution)/shard_map/pallas_call | solution.py:509
  37.7 4.5 %fusion.2 = (bf16[2,34,96,128]{3,2,1,0:T(8,128)(2,1)}, bf16[2,34,96,128]{3,2,1,0:T(8,128)(2,1)}) fusion(bf16[4,34,96,128]{3,2,1,0:T(8,128)(2,1)} %get-tuple-element.26), kind=kLoop, calls=%fused_computation.16 | loop fusion | bytes 6684672 | tf_op jit(solution)/shard_map/slice | solution.py:602
  42.2 2.3 %fusion.3 = (bf16[4,34,48,128]{3,2,1,0:T(8,128)(2,1)}, bf16[4,34,48,128]{3,2,1,0:T(8,128)(2,1)}) fusion(bf16[8,34,48,128]{3,2,1,0:T(8,128)(2,1)S(1)} %copy-done), kind=kLoop, calls=%fused_computation.17 | loop fusion | bytes 6684672 | tf_op jit(solution)/shard_map/slice | solution.py:602
  44.5 0.5 copy-done.2
  45.0 1.6 %fusion.4 = (f32[2,2,32,16,128]{4,3,2,1,0:T(8,128)}, f32[2,2,32,16,128]{4,3,2,1,0:T(8,128)}) fusion(f32[2,6,32,16,128]{4,3,2,1,0:T(8,128)S(1)} %copy-done.2), kind=kLoop, calls=%fused_computation.18 | loop fusion | bytes 4194304 | tf_op jit(solution)/shard_map/slice | solution.py:602
  46.6 0.7 copy-done.1
  47.3 1.5 %fusion.6 = (f32[4,32,16,128]{3,2,1,0:T(8,128)}, f32[4,32,16,128]{3,2,1,0:T(8,128)}) fusion(f32[8,32,16,128]{3,2,1,0:T(8,128)S(1)} %copy-done.1), kind=kLoop, calls=%fused_computation.20 | loop fusion | bytes 4194304 | tf_op jit(solution)/shard_map/slice | solution.py:602
  48.8 0.9 copy-done.3
  49.8 1.5 %fusion.5 = (bf16[2,34,48,128]{3,2,1,0:T(8,128)(2,1)}, bf16[2,34,48,128]{3,2,1,0:T(8,128)(2,1)}) fusion(bf16[6,34,48,128]{3,2,1,0:T(8,128)(2,1)S(1)} %copy-done.3), kind=kLoop, calls=%fused_computation.19 | loop fusion | bytes 3342336 | tf_op jit(solution)/shard_map/slice | solution.py:602
  51.2 0.0 collective-permute-done.1.halo
  51.2 0.7 copy-done.9
  51.9 16.0 %shard_map.79 = (bf16[2,32,16,128]{3,2,1,0:T(8,128)(2,1)}, f32[4,32,16,128]{3,2,1,0:T(8,128)}, bf16[4,34,96,128]{3,2,1,0:T(8,128)(2,1)}, f32[1152,256]{1,0:T(8,128)}, f32[1152,256]{1,0:T(8,128)}) custom-call(bf16[33,32,128]{2,1,0:T(8,128)(2,1)} %copy-done.9, bf16[4,34,48,128]{3,2,1,0:T(8,128)(2,1)} %get-tuple-element.46.xv, ...), custom_call_target="tpu_custom_call" | custom-call | flops 4831838208 | bytes 16048128 | tf_op jit(solution)/shard_map/pallas_call | solution.py:509
  68.0 0.0 collective-permute-done.halo
  68.0 0.7 copy-done.8
  68.7 16.1 %shard_map.78 = (bf16[2,32,16,128]{3,2,1,0:T(8,128)(2,1)}, f32[4,32,16,128]{3,2,1,0:T(8,128)}, bf16[4,34,96,128]{3,2,1,0:T(8,128)(2,1)}, f32[1152,256]{1,0:T(8,128)}, f32[1152,256]{1,0:T(8,128)}) custom-call(bf16[33,32,128]{2,1,0:T(8,128)(2,1)} %copy-done.8, bf16[4,34,48,128]{3,2,1,0:T(8,128)(2,1)} %get-tuple-element.47.xv, ...), custom_call_target="tpu_custom_call" | custom-call | flops 4831838208 | bytes 16048128 | tf_op jit(solution)/shard_map/pallas_call | solution.py:509
  84.8 4.3 %shard_map.81 = f32[216,128]{1,0:T(8,128)} custom-call(f32[1152,256]{1,0:T(8,128)} %get-tuple-element.38.a1, f32[1152,256]{1,0:T(8,128)} %get-tuple-element.39.a2, f32[1152,256]{1,0:T(8,128)} %get-tuple-element.40.b1, f32[1152,256]{1,0:T(8,128)} %get-tuple-element.41.b2, f32[1152,256]{1,0:T(8,128)} %get-tuple-element.42.c1, f32[1152,256]{1,0:T(8,128)} %get-tuple-element.43.c2), custom_call_target="tpu_custom_call" | custom-call | bytes 7188480 | tf_op jit(solution)/shard_map/pallas_call | solution.py:509
  89.1 2.0 %collective-permute-start.4 = (f32[216,128]{1,0:T(8,128)}, f32[216,128]{1,0:T(8,128)S(1)}, u32[]{:S(2)}, u32[]{:S(2)}) collective-permute-start(f32[216,128]{1,0:T(8,128)} %shard_map.81), channel_id=1, source_target_pairs={{0,2},{1,3},{2,0},{3,1},{4,6},{5,7},{6,4},{7,5},{8,10},{9,11},{10,... | collective-permute-start | bytes 331784 | tf_op jit(solution)/shard_map/ppermute | solution.py:532
  91.1 2.9 %collective-permute-done.4 = f32[216,128]{1,0:T(8,128)S(1)} collective-permute-done((f32[216,128]{1,0:T(8,128)}, f32[216,128]{1,0:T(8,128)S(1)}, u32[]{:S(2)}, u32[]{:S(2)}) %collective-permute-start.4) | collective-permute-done | bytes 110624 | tf_op jit(solution)/shard_map/ppermute | solution.py:532
  94.1 0.9 add.22
  95.0 2.5 %collective-permute-start.5 = (f32[216,128]{1,0:T(8,128)S(1)}, f32[216,128]{1,0:T(8,128)S(1)}, u32[]{:S(2)}, u32[]{:S(2)}) collective-permute-start(f32[216,128]{1,0:T(8,128)S(1)} %add.22), channel_id=1, source_target_pairs={{0,4},{1,5},{2,6},{3,7},{4,0},{5,1},{6,2},{7,3},{8,12},{9,13},{10,... | collective-permute-start | bytes 331784 | tf_op jit(solution)/shard_map/ppermute | solution.py:532
  97.5 0.0 copy-done.10
  97.5 4.4 %collective-permute-start.2 = (bf16[2,32,16,128]{3,2,1,0:T(8,128)(2,1)S(1)}, bf16[2,32,16,128]{3,2,1,0:T(8,128)(2,1)S(1)}, u32[]{:S(2)}, u32[]{:S(2)}) collective-permute-start(bf16[2,32,16,128]{3,2,1,0:T(8,128)(2,1)S(1)} %copy-done.10), channel_id=1, source_target_pairs={{0,1},{1,2},{2,3},{3,4},{4,5},{5,6},{6,7},{7,8},{8,9},{9,10},{10,1... | collective-permute-start | bytes 786440 | tf_op jit(solution)/shard_map/ppermute | solution.py:607
  101.9 1.3 collective-permute-start.3
  103.2 0.0 collective-permute-done.5
  103.2 4.6 %collective-permute-start.6 = (f32[216,128]{1,0:T(8,128)S(1)}, f32[216,128]{1,0:T(8,128)S(1)}, u32[]{:S(2)}, u32[]{:S(2)}) collective-permute-start(f32[216,128]{1,0:T(8,128)S(1)} %add.23), channel_id=1, source_target_pairs={{0,8},{1,9},{2,10},{3,11},{4,12},{5,13},{6,14},{7,15},{8,0},{9,1},... | collective-permute-start | bytes 331784 | tf_op jit(solution)/shard_map/ppermute | solution.py:532
  107.8 8.7 %collective-permute-done.6 = f32[216,128]{1,0:T(8,128)S(1)} collective-permute-done((f32[216,128]{1,0:T(8,128)S(1)}, f32[216,128]{1,0:T(8,128)S(1)}, u32[]{:S(2)}, u32[]{:S(2)}) %collective-permute-start.6) | collective-permute-done | bytes 110624 | tf_op jit(solution)/shard_map/ppermute | solution.py:532
  116.5 0.1 collective-permute-start.7
  116.6 4.7 %collective-permute-done.7 = f32[216,128]{1,0:T(8,128)S(1)} collective-permute-done((f32[216,128]{1,0:T(8,128)S(1)}, f32[216,128]{1,0:T(8,128)S(1)}, u32[]{:S(2)}, u32[]{:S(2)}) %collective-permute-start.7) | collective-permute-done | bytes 110624 | tf_op jit(solution)/shard_map/ppermute | solution.py:532
  121.3 0.1 collective-permute-start.8
  121.4 0.0 collective-permute-done.2.lo
  121.4 0.0 collective-permute-done.3.hi
  121.5 0.7 copy-done.5
  122.1 0.1 copy-done.6
  122.2 11.8 %shard_map.80 = f32[16,8,32,128]{3,2,1,0:T(8,128)} custom-call(bf16[2,128,2304]{2,1,0:T(8,128)(2,1)} %get-tuple-element.23.mb, bf16[4,34,96,128]{3,2,1,0:T(8,128)(2,1)} %get-tuple-element.30.d1a, bf16[2,34,96,128]{3,2,1,0:T(8,128)(2,1)} %get-tuple-element.31.d1b, bf16[4,34,96,128]{3,2,1,0:T(8,128)(2,1)} %get-tuple-element.32.d1c, ...), custom_call_target="tpu_custom_call" | custom-call | flops 2415919104 | bytes 14778368 | tf_op jit(solution)/shard_map/pallas_call | solution.py:509
  134.0 0.0 collective-permute-done.8
  134.0 0.7 broadcast_select_fusion
  134.8 2.0 %shard_map.82 = f32[2,32,432]{2,1,0:T(8,128)} custom-call(f32[216,128]{1,0:T(8,128)} %get-tuple-element.61.mine, f32[216,128]{1,0:T(8,128)} %get-tuple-element.60.other, f32[1,1]{1,0:T(1,128)} %constant.16.clone.1.bound, f32[1,1]{1,0:T(1,128)} %constant.17.clone.1.scaling), custom_call_target="tpu_custom_call" | custom-call | bytes 331784 | tf_op jit(solution)/shard_map/pallas_call | solution.py:509
  (23 shorter events, 0.2 us)
Async XLA Ops:
  0.6 1.4 %copy-start.4 = (s32[1,2,8,32,128]{4,3,2,1,0:T(8,128)S(1)}, s32[1,2,8,32,128]{4,3,2,1,0:T(8,128)}, u32[]{:S(2)}) copy-start(s32[1,2,8,32,128]{4,3,2,1,0:T(8,128)} %param.8) | copy-start | bytes 786436
  2.0 7.0 %copy-start.7 = (bf16[2,32,432]{2,1,0:T(8,128)(2,1)S(1)}, bf16[2,32,432]{2,1,0:T(8,128)(2,1)}, u32[]{:S(2)}) copy-start(bf16[2,32,432]{2,1,0:T(8,128)(2,1)} %ker.1) | copy-start | bytes 165892
  2.2 49.1 %collective-permute-start.1 = (bf16[33,32,128]{2,1,0:T(8,128)(2,1)S(1)}, bf16[33,32,128]{2,1,0:T(8,128)(2,1)S(1)}, u32[]{:S(2)}, u32[]{:S(2)}) collective-permute-start(bf16[33,32,128]{2,1,0:T(8,128)(2,1)S(1)} %pad_maximum_fusion.1), channel_id=1, source_target_pairs={{1,0},{2,1},{3,2},{4,3},{5,4},{6,5},{7,6},{8,7},{9,8},{10,9},{11,1... | collective-permute-start | bytes 811016 | tf_op jit(solution)/shard_map/ppermute | solution.py:549
  3.5 64.5 %collective-permute-start = (bf16[33,32,128]{2,1,0:T(8,128)(2,1)S(1)}, bf16[33,32,128]{2,1,0:T(8,128)(2,1)S(1)}, u32[]{:S(2)}, u32[]{:S(2)}) collective-permute-start(bf16[33,32,128]{2,1,0:T(8,128)(2,1)S(1)} %pad_maximum_fusion), channel_id=1, source_target_pairs={{0,1},{1,2},{2,3},{3,4},{4,5},{5,6},{6,7},{7,8},{8,9},{9,10},{10,1... | collective-permute-start | bytes 811016 | tf_op jit(solution)/shard_map/ppermute | solution.py:548
  37.7 4.5 %copy-start = (bf16[8,34,48,128]{3,2,1,0:T(8,128)(2,1)S(1)}, bf16[8,34,48,128]{3,2,1,0:T(8,128)(2,1)}, u32[]{:S(2)}) copy-start(bf16[8,34,48,128]{3,2,1,0:T(8,128)(2,1)} %get-tuple-element.24) | copy-start | bytes 10027012
  42.2 2.8 %copy-start.2 = (f32[2,6,32,16,128]{4,3,2,1,0:T(8,128)S(1)}, f32[2,6,32,16,128]{4,3,2,1,0:T(8,128)}, u32[]{:S(2)}) copy-start(f32[2,6,32,16,128]{4,3,2,1,0:T(8,128)} %get-tuple-element.27) | copy-start | bytes 9437188
  44.9 2.3 %copy-start.1 = (f32[8,32,16,128]{3,2,1,0:T(8,128)S(1)}, f32[8,32,16,128]{3,2,1,0:T(8,128)}, u32[]{:S(2)}) copy-start(f32[8,32,16,128]{3,2,1,0:T(8,128)} %get-tuple-element.28) | copy-start | bytes 6291460
  47.3 2.5 %copy-start.3 = (bf16[6,34,48,128]{3,2,1,0:T(8,128)(2,1)S(1)}, bf16[6,34,48,128]{3,2,1,0:T(8,128)(2,1)}, u32[]{:S(2)}) copy-start(bf16[6,34,48,128]{3,2,1,0:T(8,128)(2,1)} %get-tuple-element.25) | copy-start | bytes 7520260
  51.2 0.7 copy-start.9
  68.0 0.7 copy-start.8
  84.8 12.6 %copy-start.10 = (bf16[2,32,16,128]{3,2,1,0:T(8,128)(2,1)S(1)}, bf16[2,32,16,128]{3,2,1,0:T(8,128)(2,1)}, u32[]{:S(2)}) copy-start(bf16[2,32,16,128]{3,2,1,0:T(8,128)(2,1)} %get-tuple-element.36) | copy-start | bytes 786436
  84.8 17.0 %copy-start.11 = (bf16[2,32,16,128]{3,2,1,0:T(8,128)(2,1)S(1)}, bf16[2,32,16,128]{3,2,1,0:T(8,128)(2,1)}, u32[]{:S(2)}) copy-start(bf16[2,32,16,128]{3,2,1,0:T(8,128)(2,1)} %get-tuple-element.37) | copy-start | bytes 786436
  89.1 5.0 %collective-permute-start.4 = (f32[216,128]{1,0:T(8,128)}, f32[216,128]{1,0:T(8,128)S(1)}, u32[]{:S(2)}, u32[]{:S(2)}) collective-permute-start(f32[216,128]{1,0:T(8,128)} %shard_map.81), channel_id=1, source_target_pairs={{0,2},{1,3},{2,0},{3,1},{4,6},{5,7},{6,4},{7,5},{8,10},{9,11},{10,... | collective-permute-start | bytes 331784 | tf_op jit(solution)/shard_map/ppermute | solution.py:532
  95.0 8.2 %collective-permute-start.5 = (f32[216,128]{1,0:T(8,128)S(1)}, f32[216,128]{1,0:T(8,128)S(1)}, u32[]{:S(2)}, u32[]{:S(2)}) collective-permute-start(f32[216,128]{1,0:T(8,128)S(1)} %add.22), channel_id=1, source_target_pairs={{0,4},{1,5},{2,6},{3,7},{4,0},{5,1},{6,2},{7,3},{8,12},{9,13},{10,... | collective-permute-start | bytes 331784 | tf_op jit(solution)/shard_map/ppermute | solution.py:532
  97.5 24.0 %collective-permute-start.2 = (bf16[2,32,16,128]{3,2,1,0:T(8,128)(2,1)S(1)}, bf16[2,32,16,128]{3,2,1,0:T(8,128)(2,1)S(1)}, u32[]{:S(2)}, u32[]{:S(2)}) collective-permute-start(bf16[2,32,16,128]{3,2,1,0:T(8,128)(2,1)S(1)} %copy-done.10), channel_id=1, source_target_pairs={{0,1},{1,2},{2,3},{3,4},{4,5},{5,6},{6,7},{7,8},{8,9},{9,10},{10,1... | collective-permute-start | bytes 786440 | tf_op jit(solution)/shard_map/ppermute | solution.py:607
  101.9 19.6 %collective-permute-start.3 = (bf16[2,32,16,128]{3,2,1,0:T(8,128)(2,1)S(1)}, bf16[2,32,16,128]{3,2,1,0:T(8,128)(2,1)S(1)}, u32[]{:S(2)}, u32[]{:S(2)}) collective-permute-start(bf16[2,32,16,128]{3,2,1,0:T(8,128)(2,1)S(1)} %copy-done.11), channel_id=1, source_target_pairs={{1,0},{2,1},{3,2},{4,3},{5,4},{6,5},{7,6},{8,7},{9,8},{10,9},{11,1... | collective-permute-start | bytes 786440 | tf_op jit(solution)/shard_map/ppermute | solution.py:606
  103.2 13.3 %collective-permute-start.6 = (f32[216,128]{1,0:T(8,128)S(1)}, f32[216,128]{1,0:T(8,128)S(1)}, u32[]{:S(2)}, u32[]{:S(2)}) collective-permute-start(f32[216,128]{1,0:T(8,128)S(1)} %add.23), channel_id=1, source_target_pairs={{0,8},{1,9},{2,10},{3,11},{4,12},{5,13},{6,14},{7,15},{8,0},{9,1},... | collective-permute-start | bytes 331784 | tf_op jit(solution)/shard_map/ppermute | solution.py:532
  116.5 4.8 %collective-permute-start.7 = (f32[216,128]{1,0:T(8,128)S(1)}, f32[216,128]{1,0:T(8,128)S(1)}, u32[]{:S(2)}, u32[]{:S(2)}) collective-permute-start(f32[216,128]{1,0:T(8,128)S(1)} %add.24), channel_id=1, source_target_pairs={{0,1},{1,0},{2,3},{3,2},{4,5},{5,4},{6,7},{7,6},{8,9},{9,8},{10,11... | collective-permute-start | bytes 331784 | tf_op jit(solution)/shard_map/ppermute | solution.py:532
  121.3 12.7 %collective-permute-start.8 = (f32[216,128]{1,0:T(8,128)S(1)}, f32[216,128]{1,0:T(8,128)S(1)}, u32[]{:S(2)}, u32[]{:S(2)}) collective-permute-start(f32[216,128]{1,0:T(8,128)S(1)} %add.25), channel_id=1, source_target_pairs={{0,16},{16,0},{1,17},{17,1},{2,18},{18,2},{3,19},{19,3},{4,20},{20... | collective-permute-start | bytes 331784 | tf_op jit(solution)/shard_map/ppermute | solution.py:613
  121.4 0.7 copy-start.5
  121.4 0.8 copy-start.6

commit v2 on v0

v2 whole, which is shorter than its diff:
```python
import functools
import jax
import jax.numpy as jnp
import numpy as np
from jax import lax
from jax.experimental import pallas as pl
from jax.experimental.pallas import tpu as pltpu
from jax.sharding import PartitionSpec as P

F32, BF16 = jnp.float32, jnp.bfloat16
PZ, PH = 2, 4
PF = 2
STEP = 8
WZ, WH = PZ + 2, PH + 2
VMEM = pltpu.VMEM


def with_halo(array, sides, width):
    for axis, dim in sides:
        peers, length = (lax.axis_size(axis), array.shape[dim])
        up = [(i, (i + 1) % peers) for i in range(peers - 1)]
        down = [(j, i) for i, j in up]
        last = lax.slice_in_dim(array, length - width, length, axis=dim)
        leading = lax.slice_in_dim(array, 0, width, axis=dim)
        before = lax.ppermute(last, axis, up)
        after = lax.ppermute(leading, axis, down)
        array = jnp.concatenate([before, array, after], axis=dim)
    return array


def shifted_stack(extended, flip):
    zs = extended.shape[2] - 2
    hs, ws = (extended.shape[3], extended.shape[4])
    padded = jnp.pad(extended, ((0, 0), (0, 0), (0, 0), (1, 1), (1, 1)))
    taps = []
    for tap in range(27):
        dz, dh, dw = tap // 9, tap // 3 % 3, tap % 3
        if flip:
            dz, dh, dw = 2 - dz, 2 - dh, 2 - dw
        taps.append(padded[:, :, dz : dz + zs, dh : dh + hs, dw : dw + ws])
    return jnp.stack(taps, axis=1)


def layer_forward(field, kernel):
    patches = shifted_stack(with_halo(field, (("slab", 2),), 1), False)
    ex, taps, chans, zs, hs, ws = patches.shape
    patches = patches.reshape((ex, taps * chans, zs, hs, ws))
    pre = jnp.einsum("ok,ekzhw->eozhw", kernel, patches, preferred_element_type=F32)
    return (pre, patches)


def layer_backward(delta, kernel, patches):
    grads = jnp.einsum("eozhw,ekzhw->eok", delta, patches, preferred_element_type=F32)
    extended = with_halo(delta, (("slab", 2),), 1)
    shaped = kernel.reshape((kernel.shape[0], 27, kernel.shape[1] // 27))
    spread = jnp.einsum(
        "otc,etozhw->eczhw", shaped, shifted_stack(extended, True), preferred_element_type=F32
    )
    return (grads, spread)


def plain_device(volume, cotangent, gate_mask, loss_scale, canary, kernels):
    chans = volume.shape[1]
    local_ex = volume.shape[0]
    mask_one = gate_mask[:, 0][:, None].astype(F32)
    mask_two = gate_mask[:, 1][:, None].astype(F32)
    pre_one, patches_one = layer_forward(volume, kernels[0])
    value_one = pre_one[:, :chans]
    sig_one = jax.nn.sigmoid(pre_one[:, chans:])
    hidden = (volume.astype(F32) + value_one * sig_one * mask_one).astype(BF16)
    pre_two, patches_two = layer_forward(hidden, kernels[1])
    value_two = pre_two[:, :chans]
    sig_two = jax.nn.sigmoid(pre_two[:, chans:])
    weights = channel_weights(chans, loss_scale, canary)
    grad_out = cotangent.astype(F32) * weights[:, :, None, None, None]
    delta_two = jnp.concatenate(
        [
            grad_out * sig_two * mask_two,
            grad_out * value_two * sig_two * (1.0 - sig_two) * mask_two,
        ],
        axis=1,
    ).astype(BF16)
    grad_two, spread_two = layer_backward(delta_two, kernels[1], patches_two)
    grad_hidden = grad_out + spread_two
    delta_one = jnp.concatenate(
        [
            grad_hidden * sig_one * mask_one,
            grad_hidden * value_one * sig_one * (1.0 - sig_one) * mask_one,
        ],
        axis=1,
    ).astype(BF16)
    grad_one, spread_one = layer_backward(delta_one, kernels[0], patches_one)
    input_grad = grad_hidden + spread_one
    flat = jnp.stack([grad_one, grad_two], axis=1).reshape((local_ex, -1))
    bound, scaling = clip_numbers(volume, kernels)
    summed = lax.psum(flat, "slab")
    norm = jnp.sqrt(jnp.sum(summed * summed, axis=1) + 1e-06)
    factor = jnp.minimum(1.0, bound / norm)
    total = lax.psum(jnp.sum(summed * factor[:, None], axis=0), "ex")
    return (input_grad, (total * scaling).reshape(kernels.shape))


def channel_weights(chans, loss_scale, canary):
    ids = jnp.arange(chans, dtype=jnp.int32)
    return (1.0 + 2.0 * (ids[None, :] == canary[:, None]).astype(F32)) * loss_scale[:, None]


def clip_numbers(volume, kernels, sqrt=jnp.sqrt, one=F32):
    chans = volume.shape[1]
    depth = volume.shape[2] * lax.axis_size("slab")
    bound = 20.0 * sqrt(one(depth * volume.shape[3] * volume.shape[4]))
    examples = volume.shape[0] * lax.axis_size("ex")
    scaling = sqrt(one(108 * chans * chans)) / (bound * sqrt(one(examples)))
    return bound, scaling


def side_shifts(tile):
    lane = lax.broadcasted_iota(jnp.int32, tile.shape, tile.ndim - 1)
    last = tile.shape[-1] - 1
    before = jnp.where(lane == 0, 0.0, pltpu.roll(tile, 1, tile.ndim - 1))
    after = jnp.where(lane == last, 0.0, pltpu.roll(tile, last, tile.ndim - 1))
    return before, after


def put_rows(ref, plane, h, tile):
    rows, chans = tile.shape[:2]
    before, after = side_shifts(tile)
    for s, part in enumerate((before, tile, after)):
        ref[plane, pl.ds(h + 1, rows), s * chans : (s + 1) * chans, :] = part.astype(BF16)


def put_half(ref, plane, h, tile, which):
    rows, chans = tile.shape[:2]
    before, after = side_shifts(tile)
    for s, part in enumerate((before, tile, after)):
        at = (s * 2 + which) * chans
        ref[plane, pl.ds(h + 1, rows), at : at + chans, :] = part.astype(BF16)


def clear_edges(ref):
    for plane in range(ref.shape[0]):
        zero = jnp.zeros(ref.shape[2:], BF16)
        ref[plane, 0] = zero
        ref[plane, ref.shape[1] - 1] = zero


def windows(planes, blocks, ph):
    cols = []
    for h in blocks:
        parts = []
        for ref, at in planes:
            part = ref[at, pl.ds(h, ph + 2)]
            parts.append(part.reshape((-1, part.shape[-1])))
        cols.append(jnp.concatenate(parts, axis=0))
    return jnp.concatenate(cols, axis=1)


def conv_blocks(mat, planes, h, ph=PH):
    out = jnp.dot(mat, windows(planes, range(h, h + STEP, ph), ph), preferred_element_type=F32)
    return out.reshape((PZ * ph, -1, out.shape[-1]))


def split_blocks(tile, fn):
    ph = tile.shape[0] // PZ
    blocks = STEP // ph
    width = tile.shape[-1] // blocks
    for pz in range(PZ):
        for b in range(blocks):
            fn(pz, b * ph, tile[pz * ph : (pz + 1) * ph, :, b * width : (b + 1) * width])


def join_blocks(fn, ph):
    planes = []
    for pz in range(PZ):
        planes.append(jnp.concatenate([fn(pz, row) for row in range(0, STEP, ph)], axis=2))
    return jnp.concatenate(planes, axis=0)


def mask_blocks(mask_planes, h, chans, ph):
    parts = []
    for pz in range(PZ):
        ref, at = mask_planes[pz]
        rows = ref[at + (pl.ds(h, STEP),)].astype(F32)
        both = jnp.concatenate([rows[row : row + ph] for row in range(0, STEP, ph)], axis=1)
        parts.append(jnp.broadcast_to(both[:, None, :], (ph, chans, both.shape[1])))
    return jnp.concatenate(parts, axis=0)


def row_loop(hs, body):
    for h in range(0, hs, STEP):
        body(h)


def forward_one(mat_ref, v_planes, v_centre, mask_planes, x1, x1_at, gates, gates_at, hs, chans):
    def body(h):
        pre = conv_blocks(mat_ref[...], v_planes, h, PF)
        val, sig = pre[:, :chans], jax.nn.sigmoid(pre[:, chans:])
        mask = mask_blocks(mask_planes, h, chans, PF)

        def centre(pz, row):
            ref, at = v_centre[pz]
            return ref[at, pl.ds(h + row + 1, PF), chans : 2 * chans, :].astype(F32)

        open_ = sig * mask
        hid = join_blocks(centre, PF) + val * open_
        slope = val * open_ * (1.0 - sig)
        split_blocks(hid, lambda pz, row, t: put_rows(x1, x1_at + pz, h + row, t))

        def keep(which):
            def put(pz, row, t):
                gates[which, gates_at + pz, pl.ds(h + row, PF)] = t

            return put

        split_blocks(open_, keep(0))
        split_blocks(slope, keep(1))

    row_loop(hs, body)


def forward_two(mat_ref, x1_planes, mask_planes, dy_fn, d2, d2_at, hs, chans):
    def body(h):
        pre = conv_blocks(mat_ref[...], x1_planes, h, PF)
        val, sig = pre[:, :chans], jax.nn.sigmoid(pre[:, chans:])
        dy = join_blocks(lambda pz, row: dy_fn(pz, h + row, PF), PF)
        top = dy * sig * mask_blocks(mask_planes, h, chans, PF)
        low = top * val * (1.0 - sig)
        split_blocks(top, lambda pz, row, t: put_half(d2, d2_at + pz, h + row, t, 0))
        split_blocks(low, lambda pz, row, t: put_half(d2, d2_at + pz, h + row, t, 1))

    row_loop(hs, body)


def backward_two(mat, d2_planes, dy_fn, gates, gates_at, dx, dx_at, d1, d1_at, hs):
    def body(h):
        def each(pz, row, part):
            row = h + row
            if dy_fn[pz] is not None:
                part = part + dy_fn[pz](row)
            dx[dx_at + pz, pl.ds(row, PH)] = part
            for which in range(2):
                gate = gates[which, gates_at + pz, pl.ds(row, PH)]
                put_half(d1, d1_at + pz, row, part * gate, which)

        split_blocks(conv_blocks(mat(), d2_planes, h), each)

    row_loop(hs, body)


def weight_blocks(x_planes, d_planes, acc, hs):
    blocks = tuple(range(0, hs, PH))
    lhs = windows(x_planes, blocks, PH)
    cols = []
    for h in blocks:
        parts = []
        for ref, at in d_planes:
            outs = ref.shape[2] // 3
            parts.append(ref[at, h + 1 : h + 1 + PH, outs : 2 * outs, :].reshape((PH * outs, -1)))
        cols.append(jnp.concatenate(parts, axis=0))
    rhs = jnp.concatenate(cols, axis=1)
    acc[...] += lax.dot_general(lhs, rhs, (((1,), (1,)), ((), ())), preferred_element_type=F32)


def fold_blocks(acc, outs, chans):
    taps = 9 * chans
    width = PH * outs
    rows = WH * 3 * chans
    total = None
    for ph in range(PH):
        part = None
        for pz in range(PZ):
            pieces = []
            for dz in range(3):
                at = (pz + dz) * rows + ph * 3 * chans
                pieces.append(acc[at : at + taps, pz * width : (pz + 1) * width])
            piece = jnp.concatenate(pieces, axis=0)
            part = piece if part is None else part + piece
        if ph:
            part = pltpu.roll(part, width - ph * outs, 1)
        total = part if total is None else total + part
    return total


def place_matrix(cols, stride, total, piece):
    k = lax.broadcasted_iota(jnp.int32, (cols, total), 0)
    j = lax.broadcasted_iota(jnp.int32, (cols, total), 1)
    group = (k >= piece).astype(jnp.int32) + (k >= 2 * piece).astype(jnp.int32)
    return (j == k + group * (stride - piece)).astype(F32).astype(BF16)


def spread_kernel(rows, out_ref, layer, width, ph):
    outs, cols = rows.shape
    stride = (ph + 2) * width
    place = place_matrix(cols, stride, WZ * stride, 3 * width)
    base = jnp.dot(rows, place, preferred_element_type=F32)
    for pz in range(PZ):
        for p in range(ph):
            at = (pz * ph + p) * outs
            shift = pz * stride + p * width
            tile = pltpu.roll(base, shift, 1) if shift else base
            out_ref[layer, at : at + outs, :] = tile.astype(BF16)


def to_rows(source, scratch, put):
    chans, hs, ws = source.shape
    scratch[...] = source.astype(F32).reshape((chans * hs, ws))
    for h in range(hs):
        put(h, scratch[pl.ds(h, chans, stride=hs), :])


def flip_kernel(kernel, chans):
    turned = kernel.astype(F32).T
    pieces = [turned[t * chans : (t + 1) * chans] for t in reversed(range(27))]
    return jnp.concatenate(pieces, axis=1).astype(BF16)


def folded(acc, chans):
    outs = 2 * chans
    one, two = (fold_blocks(acc.at[layer], outs, chans) for layer in range(2))
    lane = lax.broadcasted_iota(jnp.int32, one.shape, 1)
    both = jnp.where(lane < outs, one, pltpu.roll(two, outs, 1))
    half = both.shape[0] // 2
    lane = lax.broadcasted_iota(jnp.int32, (half, both.shape[1]), 1)
    return jnp.where(lane < 2 * outs, both[:half], pltpu.roll(both[half:], 2 * outs, 1))


def pack_kernel(vol, mask, up, down):
    chans, zs = vol.shape[1:3]
    for out, first, edge in ((up, zs - 2, zs - 1), (down, 0, 0)):
        for i in range(2):
            out[i * chans : (i + 1) * chans] = vol[0, :, first + i]
        out[2 * chans] = mask[0, 0, edge].astype(F32).astype(BF16)


def arrange_kernel(vol, xv, rows):
    clear_edges(xv)

    def arrange(z, carry):
        to_rows(vol[0, :, z], rows, lambda h, t: put_rows(xv, z, h, t[None]))
        return carry

    lax.fori_loop(0, xv.shape[0], arrange, 0)


def first_kernel(xv, cot, mask, scale, canary, ker, mf, mb, ct, x1, g1, d2, total, rows, acc):
    chans, zs, hs, ws = cot.shape[1:]
    for layer in range(2):
        spread_kernel(ker[layer], mf, layer, 3 * chans, PF)
        spread_kernel(flip_kernel(ker[layer], chans), mb, layer, 6 * chans, PH)
    clear_edges(x1)
    clear_edges(d2)
    ids = lax.broadcasted_iota(jnp.int32, (chans, ws), 0)
    weights = jnp.where(ids == canary[...], 3.0, 1.0) * scale[...]

    def scaled(z, carry):
        def put(h, t):
            ct[z, h] = t * weights

        to_rows(cot[0, :, z], rows, put)
        return carry

    lax.fori_loop(0, zs, scaled, 0)

    def layer_one(k, carry):
        z = 2 * k + 1
        forward_one(
            mf.at[0],
            [(xv, z - 1 + i) for i in range(WZ)],
            [(xv, z + i) for i in range(PZ)],
            [(mask, (0, 0, z + i)) for i in range(PZ)],
            x1, 2 * k, g1, 2 * k, hs, chans,
        )
        return carry

    lax.fori_loop(0, (zs - 2) // 2, layer_one, 0)
    acc[...] = jnp.zeros_like(acc)

    def layer_two(k, carry):
        z = 2 * k + 2
        x_planes = [(x1, z - 2 + i) for i in range(WZ)]
        forward_two(
            mf.at[1], x_planes, [(mask, (0, 1, z + i)) for i in range(PZ)],
            lambda pz, h, n: ct[z + pz, pl.ds(h, n)], d2, z, hs, chans,
        )
        weight_blocks(x_planes, two(d2, z), acc.at[1], hs)
        return carry

    lax.fori_loop(0, (zs - 4) // 2, layer_two, 0)
    total[...] = folded(acc, chans)


def two(ref, at):
    return [(ref, at), (ref, at + 1)]


def edge_parts(low, halo, xv, x1, mask, ct, mf, mb, send, dx, d1, d2, d2_at, xh, x1h, gh, rows, acc):
    zs, chans, hs = xv.shape[0], xv.shape[2] // 3, xv.shape[1] - 2
    clear_edges(xh)
    clear_edges(x1h)
    for i in range(2):
        to_rows(halo[i * chans : (i + 1) * chans], rows, lambda h, t: put_rows(xh, i, h, t[None]))
    outer = (halo, (2 * chans,))
    if low:
        v_planes = two(xh, 0) + two(xv, 0)
        masks1 = [outer, (mask, (0, 0, 0))]
        x_planes = two(x1h, 0) + two(x1, 0)
        half = slice(mb.shape[2] // 2, mb.shape[2])
        dys = [None, lambda h: ct[0, pl.ds(h, PH)]]
        first, outside = 0, 0
    else:
        v_planes = two(xv, zs - 2) + two(xh, 0)
        masks1 = [(mask, (0, 0, zs - 1)), outer]
        x_planes = two(x1, zs - 4) + two(x1h, 0)
        half = slice(0, mb.shape[2] // 2)
        dys = [lambda h: ct[zs - 1, pl.ds(h, PH)], None]
        first, outside = zs - 2, 1
    masks2 = [(mask, (0, 1, first + i)) for i in range(PZ)]
    forward_one(mf.at[0], v_planes, v_planes[1:3], masks1, x1h, 0, gh, 0, hs, chans)
    forward_two(
        mf.at[1], x_planes, masks2, lambda pz, h, n: ct[first + pz, pl.ds(h, n)], d2, d2_at, hs, chans
    )
    backward_two(lambda: mb[1, :, half], two(d2, d2_at), dys, gh, 0, dx, 0, d1, 0, hs)

    def spread(h):
        def each(pz, row, part):
            if pz == 1 - outside:
                part = part + dx[outside, pl.ds(h + row, PH)]
            send[pz, pl.ds(h + row, PH)] = part.astype(BF16)

        split_blocks(conv_blocks(mb[0, :, half], two(d1, 0), h), each)

    row_loop(hs, spread)
    acc[...] = jnp.zeros_like(acc)
    weight_blocks(x_planes, two(d2, d2_at), acc.at[1], hs)
    weight_blocks(v_planes, two(d1, 0), acc.at[0], hs)


def low_kernel(halo, xv, x1, mask, ct, mf, mb, before, d2_in, send, dx, d1, d2, total, xh, x1h, gh, rows, acc):
    clear_edges(d1)
    edge_parts(True, halo, xv, x1, mask, ct, mf, mb, send, dx, d1, d2, 0, xh, x1h, gh, rows, acc)
    total[...] = before[...] + folded(acc, xv.shape[2] // 3)


def middle_kernel(xv, g1, ct, mb, d2, before, dx, d1, total, acc):
    zs, chans, hs = xv.shape[0], xv.shape[2] // 3, xv.shape[1] - 2
    clear_edges(d1)
    acc[...] = jnp.zeros_like(acc)

    def layer_back(k, carry):
        z = 2 * k + 1
        dys = [lambda h, i=i: ct[z + i, pl.ds(h, PH)] for i in range(PZ)]
        backward_two(
            lambda: mb[1], [(d2, z - 1 + i) for i in range(WZ)], dys, g1, z - 1, dx, 2 * k, d1, 2 * k, hs
        )
        weight_blocks([(xv, z - 1 + i) for i in range(WZ)], two(d1, 2 * k), acc.at[0], hs)
        return carry

    lax.fori_loop(0, (zs - 4) // 2, layer_back, 0)
    total[...] = before[...] + folded(acc, chans)


def high_kernel(halo, xv, x1, g1, mask, ct, mf, mb, d2, before,
                send, dx, d1, dxn, d1n, total, xh, x1h, d2h, gh, rows, acc):
    zs, chans, hs = xv.shape[0], xv.shape[2] // 3, xv.shape[1] - 2
    for ref in (d1, d1n, d2h):
        clear_edges(ref)
    edge_parts(False, halo, xv, x1, mask, ct, mf, mb, send, dx, d1, d2h, 0, xh, x1h, gh, rows, acc)
    z = zs - 3
    dys = [lambda h, i=i: ct[z + i, pl.ds(h, PH)] for i in range(PZ)]
    backward_two(lambda: mb[1], two(d2, zs - 4) + two(d2h, 0), dys, g1, z - 1, dxn, 0, d1n, 0, hs)
    weight_blocks([(xv, z - 1 + i) for i in range(WZ)], two(d1n, 0), acc.at[0], hs)
    total[...] = before[...] + folded(acc, chans)


def output_kernel(picks, extra_at, mb, *refs):
    out, token, rows = refs[-3:]
    extra = None if extra_at is None else refs[extra_at]
    chans, hs, ws = out.shape[1], out.shape[3], out.shape[4]
    d_planes = [(refs[i], at) for i, at in picks[:WZ]]
    dxs = [(refs[i], at) for i, at in picks[WZ:]]

    def body(h):
        def each(pz, row, part):
            row = h + row
            ref, at = dxs[pz]
            part = part + ref[at, pl.ds(row, PH)]
            if extra is not None:
                part = part + extra[pz, pl.ds(row, PH)].astype(F32)
            rows[pz, pl.ds(row * chans, PH * chans), :] = part.reshape((PH * chans, ws))

        split_blocks(conv_blocks(mb[0], d_planes, h), each)

    row_loop(hs, body)
    for pz in range(PZ):
        for c in range(chans):
            out[0, c, pz] = rows[pz, pl.ds(c, hs, stride=chans), :]
    token[...] = rows[0, :8, :]


def clip_kernel(bound, scaling, mine, other, out):
    total = None
    for ref in (mine, other):
        value = ref[...]
        norm = jnp.sqrt(jnp.sum(value * value, keepdims=True) + 1e-06)
        part = value * jnp.minimum(1.0, bound / norm)
        total = part if total is None else total + part
    total = total * scaling
    outs = out.shape[1]
    half = total.shape[0]
    flat = total.T
    for layer in range(2):
        for part in range(2):
            at = (part * 2 + layer) * outs
            out[layer, :, part * half : (part + 1) * half] = flat[at : at + outs]


def call(body, outs, scratch=(), flops=0, vmem=16 << 20, scalars=(), aliases=()):
    def run(*args):
        size = sum(a.size * a.dtype.itemsize for a in args) + sum(o.size * o.dtype.itemsize for o in outs)
        spaces = [pltpu.SMEM if i in scalars else VMEM for i in range(len(args))]
        return pl.pallas_call(
            body,
            out_shape=outs,
            in_specs=[pl.BlockSpec(memory_space=space) for space in spaces],
            scratch_shapes=list(scratch),
            input_output_aliases=dict(aliases),
            compiler_params=pltpu.CompilerParams(vmem_limit_bytes=vmem),
            cost_estimate=pl.CostEstimate(flops=flops, bytes_accessed=size, transcendentals=0),
        )(*args)

    return run


def shape(*dims, dtype=F32):
    return jax.ShapeDtypeStruct(dims, dtype)


def output_planes(like, z, mb, d_planes, dxs, extra, buffer, after, flops=0):
    chans, zs, hs, ws = like.shape[1:]
    arrays, picks = [], []
    for array, at in d_planes + dxs:
        where = [i for i, a in enumerate(arrays) if a is array]
        if not where:
            arrays.append(array)
        picks.append((where[0] if where else len(arrays) - 1, at))
    operands = [mb] + arrays + ([] if extra is None else [extra])
    specs = [pl.BlockSpec(memory_space=VMEM)] * len(operands)
    unread = after if buffer is None else after + [buffer]
    aliases = {} if buffer is None else {len(operands) + len(after): 0}
    body = functools.partial(output_kernel, tuple(picks), None if extra is None else len(arrays))
    return pl.pallas_call(
        body,
        grid=(1,),
        out_shape=[shape(*like.shape), shape(8, ws)],
        in_specs=specs + [pl.BlockSpec(memory_space=pl.ANY)] * len(unread),
        out_specs=[
            pl.BlockSpec((1, chans, PZ, hs, ws), lambda i: (0, 0, z // PZ, 0, 0)),
            pl.BlockSpec(memory_space=VMEM),
        ],
        scratch_shapes=[VMEM((PZ, chans * hs, ws), F32)],
        input_output_aliases=aliases,
        compiler_params=pltpu.CompilerParams(vmem_limit_bytes=16 << 20),
        cost_estimate=pl.CostEstimate(flops=flops, bytes_accessed=0, transcendentals=0),
    )(*operands, *unread)


def add_kernel(mine, other, *refs):
    refs[-1][...] = mine[...] + other[...]


def add_after(mine, other, tokens):
    return pl.pallas_call(
        add_kernel,
        out_shape=shape(*mine.shape),
        in_specs=[pl.BlockSpec(memory_space=VMEM)] * 2 + [pl.BlockSpec(memory_space=pl.ANY)] * len(tokens),
        out_specs=pl.BlockSpec(memory_space=VMEM),
        compiler_params=pltpu.CompilerParams(vmem_limit_bytes=4 << 20),
    )(mine, other, *tokens)


def block_device(volume, cotangent, gate_mask, loss_scale, canary, kernels):
    chans, zs, hs, ws = volume.shape[1:]
    outs = 2 * chans
    peers = lax.axis_size("slab")
    up = [(i, i + 1) for i in range(peers - 1)]
    down = [(i + 1, i) for i in range(peers - 1)]

    payload = shape(2 * chans + 1, hs, ws, dtype=BF16)
    going_up, going_down = call(pack_kernel, [payload, payload])(volume, gate_mask)
    below = lax.ppermute(going_up, "slab", up)
    above = lax.ppermute(going_down, "slab", down)

    k_fwd, k_bwd = WZ * (PF + 2) * 3 * chans, WZ * WH * 3 * outs
    m_fwd, m_bwd = PZ * PF * outs, PZ * PH * chans
    x_plane, d_plane, c_plane = (hs + 2, 3 * chans, ws), (hs + 2, 3 * outs, ws), (hs, chans, ws)
    total = shape(27 * chans // 2, 4 * outs)
    rows = VMEM((chans * hs, ws), F32)
    acc = VMEM((2, WZ * WH * 3 * chans, PZ * PH * outs), F32)
    pair = 2 * k_bwd * m_bwd * hs // PH * ws

    def d_planes(n):
        return shape(n, *d_plane, dtype=BF16)

    (xv,) = call(arrange_kernel, [shape(zs, *x_plane, dtype=BF16)], [rows], flops=pair * 4)(volume)
    mf, mb, ct, x1, g1, d2_in, total_in = call(
        first_kernel,
        [
            shape(2, m_fwd, k_fwd, dtype=BF16),
            shape(2, m_bwd, k_bwd, dtype=BF16),
            shape(zs, *c_plane),
            shape(zs - 2, *x_plane, dtype=BF16),
            shape(2, zs - 2, *c_plane),
            d_planes(zs - 2),
            total,
        ],
        [rows, acc],
        flops=pair * 6,
    )(xv, cotangent, gate_mask, loss_scale.reshape((1, 1)), canary.reshape((1, 1)), kernels)

    halos = [VMEM((2,) + x_plane, BF16), VMEM((2,) + x_plane, BF16)]
    gates = VMEM((2, 2) + c_plane, F32)
    send_lo, dx_lo, d1_lo, d2_lo, total_lo = call(
        low_kernel,
        [shape(2, *c_plane, dtype=BF16), shape(2, *c_plane), d_planes(2), d_planes(zs - 2), total],
        halos + [gates, rows, acc],
        flops=pair * 5,
        aliases={8: 3},
    )(below, xv, x1, gate_mask, ct, mf, mb, total_in, d2_in)
    from_above = lax.ppermute(send_lo, "slab", down)
    dx_in, d1_in, total_in = call(
        middle_kernel,
        [shape(zs - 4, *c_plane), d_planes(zs - 4), total],
        [acc],
        flops=pair * 4,
    )(xv, g1, ct, mb, d2_lo, total_lo)
    send_hi, dx_hi, d1_hi, dx_hn, d1_hn, total_hi = call(
        high_kernel,
        [
            shape(2, *c_plane, dtype=BF16),
            shape(2, *c_plane), d_planes(2), shape(2, *c_plane), d_planes(2), total,
        ],
        halos + [VMEM((2,) + d_plane, BF16), gates, rows, acc],
        flops=pair * 7,
    )(above, xv, x1, g1, gate_mask, ct, mf, mb, d2_lo, total_in)
    from_below = lax.ppermute(send_hi, "slab", up)

    def place(lo, mid, hn, hi, z):
        if z <= 0:
            return (lo, z + 1)
        if z <= zs - 4:
            return (mid, z - 1)
        return (hn, z - (zs - 3)) if z <= zs - 2 else (hi, z - (zs - 1))

    inner = list(range(2, zs - 2, 2))
    buffer = None
    mine = total_hi
    steps = [1 << i for i in range(peers.bit_length() - 1)]
    steps = steps[1:] + steps[:1]
    jobs = inner + [zs - 2, 0]
    waits = {0: [from_above]}
    for place_in_order, step in enumerate(steps):
        other = lax.ppermute(mine, "slab", [(i, i ^ step) for i in range(peers)])
        left = len(steps) - place_in_order
        now, jobs = jobs[: -(-len(jobs) // left)], jobs[-(-len(jobs) // left) :]
        tokens = []
        for z in now:
            d_list = [place(d1_lo, d1_in, d1_hn, d1_hi, z - 1 + i) for i in range(WZ)]
            dx_list = [place(dx_lo, dx_in, dx_hn, dx_hi, z + i) for i in range(PZ)]
            extra = from_above if z == zs - 2 else from_below if z == 0 else None
            buffer, token = output_planes(volume, z, mb, d_list, dx_list, extra, buffer, [mine] + waits.get(place_in_order, []))
            tokens.append(token)
        mine = add_after(mine, other, tokens)
    other = lax.ppermute(mine, "ex", [(0, 1), (1, 0)])
    numbers = [float(n) for n in clip_numbers(volume, kernels, np.sqrt, np.float32)]
    kernel_grad = call_one(functools.partial(clip_kernel, *numbers), shape(*kernels.shape), [])(mine, other)
    return (buffer, kernel_grad)


def call_one(body, out, scratch, **kwargs):
    run = call(body, [out], scratch, **kwargs)
    return lambda *args: run(*args)[0]


def per_device(*args):
    ex, chans, zs, hs, ws = args[0].shape
    blocks = ex == 1 and lax.axis_size("ex") == 2 and chans == 16 and ws == 128
    blocks = blocks and hs % 16 == 0 and zs % 2 == 0 and zs >= 8
    peers = lax.axis_size("slab")
    if blocks and peers & (peers - 1) == 0:
        return block_device(*args)
    return plain_device(*args)


def solution(mesh):
    placed = (
        P("ex", None, "slab", None, None),
        P("ex", None, "slab", None, None),
        P("ex", None, "slab", None, None),
        P("ex"),
        P("ex"),
        P(),
    )
    return jax.shard_map(
        per_device,
        mesh=mesh,
        in_specs=placed,
        out_specs=(P("ex", None, "slab", None, None), P()),
        check_vma=False,
    )
```

time: 643 us -> 65.2 us (0.10); the launches traced: 633 us -> 65 us
  local copies, waits for them, and re-layouts: 227 us -> 2.19 us
  matrix products: 189 us -> 0 us
  waiting for transfers between devices: 125 us -> 6.27 us
  other arithmetic: 52.5 us -> 0 us
  Pallas kernels: 0 us -> 31.7 us
  between operations: 16.7 us -> 2.1 us
    dot_general x6 -> x0, matrix products: 189 us -> none  [the longest x2 106 us: layer_backward(): jnp.einsum('eozhw,ekzhw->eok', delta, patches, preferred_element_type=jnp...]
    unnamed x113 -> x10, local copies, waits for them, and re-layouts: 170 us -> 2.19 us
    psum x2 -> x0, waiting for transfers between devices: 117 us -> none  [the longest x1 105 us: per_device(): summed = lax.psum(flat, 'slab')]
    another operation x6 -> x0, local copies, waits for them, and re-layouts: 52.9 us -> none  [the longest x4 49.3 us: columns(): stacked = jnp.stack(taps, axis=1)]
    pallas_call x0 -> x15, Pallas kernels: none -> 31.7 us  [the longest x7 24.5 us: run(): pl.pallas_call(body, out_shape=outs, in_specs=[pl.BlockSpec(memory_space=...]
    concatenate x4 -> x0, other arithmetic: 19.5 us -> none  [with_halo(): array = jnp.concatenate([before, array, after], axis=dim)]
    unnamed x10 -> x0, other arithmetic: 16.9 us -> none
    ppermute x8 -> x9, starting transfers between devices: 21.1 us -> 22.7 us  [the longest x4 11.5 us: block_device(): other = lax.ppermute(mine, 'slab', [(i, i ^ step) for i in range(peers)])]
  transfers between devices with their start and end apart: 10 -> 9, of which waited for: 5 -> 4; matrix products, arithmetic and copies ran while one was open for 9% -> 0% of each run, Pallas kernels for 0% -> 47%
where the time goes in v2:
time: 65.2 us; the launch traced here: 65 us
  Pallas kernels  31.7 us (49%)
  starting transfers between devices  22.7 us (35%)
  waiting for transfers between devices  6.27 us (10%)
  local copies, waits for them, and re-layouts  2.19 us (3%)
  between operations  2.1 us (3%)
    pallas_call x7, Pallas kernels, run(): pl.pallas_call(body, out_shape=outs, in_specs=[pl.BlockSpec(memory_space=...  24.5 us
    ppermute x4, starting transfers between devices, block_device(): other = lax.ppermute(mine, 'slab', [(i, i ^ step) for i in range(peers)])  11.5 us
    pallas_call x4, Pallas kernels, output_planes(): pl.pallas_call(body, grid=(1,), out_shape=[shape(*like.shape), shape(8, w...  7.13 us
    ppermute x4, waiting for transfers between devices, block_device(): other = lax.ppermute(mine, 'slab', [(i, i ^ step) for i in range(peers)])  4.96 us
    ppermute x1, starting transfers between devices, block_device(): below = lax.ppermute(going_up, 'slab', up)  4.86 us
    ppermute x1, starting transfers between devices, block_device(): from_below = lax.ppermute(send_hi, 'slab', up)  3.4 us
    unnamed x10, local copies, waits for them, and re-layouts  2.19 us
    ppermute x1, starting transfers between devices, block_device(): from_above = lax.ppermute(send_lo, 'slab', down)  1.47 us
  transfers between devices with their start and end apart: 9, of which 4 were waited for; matrix products, arithmetic and copies ran while one was open for 0% of the time, Pallas kernels for 47%

profile of v2, /device:TPU:0, one launch (start us, length us, event | category | flops | bytes accessed | tf_op | source)
XLA Modules:
  0.0 65.0 jit_solution(2398226461633864889)
XLA Ops:
  0.6 0.0 copy-start
  0.6 0.9 %copy-done = s32[1,2,8,32,128]{4,3,2,1,0:T(8,128)S(1)} copy-done((s32[1,2,8,32,128]{4,3,2,1,0:T(8,128)S(1)}, s32[1,2,8,32,128]{4,3,2,1,0:T(8,128)}, u32[]{:S(2)}) %copy-start) | copy-done | bytes 262168
  1.6 0.0 copy-start.2
  1.6 1.2 %copy-done.2 = bf16[1,16,8,32,128]{4,3,2,1,0:T(8,128)(2,1)S(1)} copy-done((bf16[1,16,8,32,128]{4,3,2,1,0:T(8,128)(2,1)S(1)}, bf16[1,16,8,32,128]{4,3,2,1,0:T(8,128)(2,1)}, u32[]{:S(2)}) %copy-start.2) | copy-done | bytes 1048600
  2.8 4.9 %collective-permute-start = (bf16[33,32,128]{2,1,0:T(8,128)(2,1)S(1)}, bf16[33,32,128]{2,1,0:T(8,128)(2,1)S(1)}, u32[]{:S(2)}, u32[]{:S(2)}) collective-permute-start(bf16[33,32,128]{2,1,0:T(8,128)(2,1)S(1)} %get-tuple-element.34), channel_id=1, source_target_pairs={{0,1},{1,2},{2,3},{3,4},{4,5},{5,6},{6,7},{7,8},{8,9},{9,10},{10,1... | collective-permute-start | bytes 811016 | tf_op jit(solution)/shard_map/ppermute | solution.py:590
  7.7 0.0 copy-start.1
  7.7 0.0 copy-start.3
  7.7 0.0 copy-start.4
  7.8 1.4 %collective-permute-start.1 = (bf16[33,32,128]{2,1,0:T(8,128)(2,1)S(1)}, bf16[33,32,128]{2,1,0:T(8,128)(2,1)S(1)}, u32[]{:S(2)}, u32[]{:S(2)}) collective-permute-start(bf16[33,32,128]{2,1,0:T(8,128)(2,1)S(1)} %get-tuple-element.47), channel_id=1, source_target_pairs={{1,0},{2,1},{3,2},{4,3},{5,4},{6,5},{7,6},{8,7},{9,8},{10,9},{11,1... | collective-permute-start | bytes 811016 | tf_op jit(solution)/shard_map/ppermute | solution.py:591
  9.2 1.9 %shard_map.77.xv = bf16[8,34,48,128]{3,2,1,0:T(8,128)(2,1)S(1)} custom-call(bf16[1,16,8,32,128]{4,3,2,1,0:T(8,128)(2,1)S(1)} %copy-done.2), custom_call_target="tpu_custom_call" | custom-call | flops 2415919104 | bytes 4390912 | tf_op jit(solution)/shard_map/pallas_call | solution.py:521
  12.4 0.0 copy-done.1
  12.4 0.0 copy-done.3
  12.4 0.0 copy-done.4
  12.4 7.7 %shard_map.78 = (bf16[2,128,768]{2,1,0:T(8,128)(2,1)S(1)}, bf16[2,128,2304]{2,1,0:T(8,128)(2,1)S(1)}, f32[8,32,16,128]{3,2,1,0:T(8,128)S(1)}, bf16[6,34,48,128]{...) custom-call(bf16[8,34,48,128]{3,2,1,0:T(8,128)(2,1)S(1)} %shard_map., ...), custom_call_target="tpu_custom_call" | custom-call | flops 3623878656 | bytes 19154952 | tf_op jit(solution)/shard_map/pallas_call | solution.py:521
  20.2 0.0 collective-permute-done.halo
  20.2 3.9 %shard_map.80 = (bf16[2,32,16,128]{3,2,1,0:T(8,128)(2,1)S(1)}, f32[2,32,16,128]{3,2,1,0:T(8,128)S(1)}, bf16[2,34,96,128]{3,2,1,0:T(8,128)(2,1)S(1)}, bf16[6,34,96,128]{3,2,1,0:T(8,128)(2,1)S(1)}, f32[216,128]{1,0:T(8,128)S(1)}) custom-call(bf16[33,32,128]{2,1,0:T(8,128)(2,1)S(1)} %collective-permute-done.halo, ...), custom_call_target="tpu_custom_call", output_to_operand_aliasing={{3}: (8, {})} | custom-call | flops 3019898880 | bytes 22757376 | tf_op jit(solution)/shard_map/pallas_call | solution.py:521
  24.0 1.5 %collective-permute-start.4 = (bf16[2,32,16,128]{3,2,1,0:T(8,128)(2,1)S(1)}, bf16[2,32,16,128]{3,2,1,0:T(8,128)(2,1)S(1)}, u32[]{:S(2)}, u32[]{:S(2)}) collective-permute-start(bf16[2,32,16,128]{3,2,1,0:T(8,128)(2,1)S(1)} %get-tuple-element.51), channel_id=1, source_target_pairs={{1,0},{2,1},{3,2},{4,3},{5,4},{6,5},{7,6},{8,7},{9,8},{10,9},{11,1... | collective-permute-start | bytes 786440 | tf_op jit(solution)/shard_map/ppermute | solution.py:629
  25.5 4.0 %shard_map.81 = (f32[4,32,16,128]{3,2,1,0:T(8,128)S(1)}, bf16[4,34,96,128]{3,2,1,0:T(8,128)(2,1)S(1)}, f32[216,128]{1,0:T(8,128)S(1)}) custom-call(bf16[8,34,48,128]{3,2,1,0:T(8,128)(2,1)S(1)} %shard_map.77.xv, f32[2,6,32,16,128]{4,3,2,1,0:T(8,128)S(1)} %get-tuple-element.41.g1, f32[8,32,16,128]{3,2,1,0:T(8,128)S(1)} %get-tuple-element.36.ct, ...), custom_call_target="tpu_custom_call" | custom-call | flops 2415919104 | bytes 19390464 | tf_op jit(solution)/shard_map/pallas_call | solution.py:521
  29.5 0.0 collective-permute-done.1.halo
  29.5 6.0 %shard_map.82 = (bf16[2,32,16,128]{3,2,1,0:T(8,128)(2,1)S(1)}, f32[2,32,16,128]{3,2,1,0:T(8,128)S(1)}, bf16[2,34,96,128]{3,2,1,0:T(8,128)(2,1)S(1)}, f32[2,32,16...) custom-call(bf16[33,32,128]{2,1,0:T(8,128)(2,1)S(1)} %collective-permute-done.1.halo, ...), custom_call_target="tpu_custom_call" | custom-call | flops 4227858432 | bytes 23085056 | tf_op jit(solution)/shard_map/pallas_call | solution.py:521
  35.5 4.8 %collective-permute-start.3 = (f32[216,128]{1,0:T(8,128)S(1)}, f32[216,128]{1,0:T(8,128)S(1)}, u32[]{:S(2)}, u32[]{:S(2)}) collective-permute-start(f32[216,128]{1,0:T(8,128)S(1)} %get-tuple-element.50.refs_2_.mine), channel_id=1, source_target_pairs={{0,2},{1,3},{2,0},{3,1},{4,6},{5,7},{6,4},{7,5},{8,10},{9,11},{10,... | collective-permute-start | bytes 331784 | tf_op jit(solution)/shard_map/ppermute | solution.py:662
  40.3 0.0 collective-permute-done.4.refs_3_.refs_4_
  40.3 1.8 %shard_map.83 = (f32[1,16,8,32,128]{4,3,2,1,0:T(8,128)}, f32[8,128]{1,0:T(8,128)S(1)}) custom-call(bf16[2,128,2304]{2,1,0:T(8,128)(2,1)S(1)} %get-tuple-element.33.mb, bf16[4,34,96,128]{3,2,1,0:T(8,128)(2,1)S(1)} %get-tuple-element.44.refs_0_.refs_1_, f32[4,32,16,128]{3,2,1,0:T(8,128)S(1)} %get-tuple-element.46.refs_1_.refs_2_.refs_3_, ...), custom_call_target="tpu_custom_call" | custom-call | tf_op jit(solution)/shard_map/pallas_call | solution.py:551
  42.1 1.0 %collective-permute-done.3.other = f32[216,128]{1,0:T(8,128)S(1)} collective-permute-done((f32[216,128]{1,0:T(8,128)S(1)}, f32[216,128]{1,0:T(8,128)S(1)}, u32[]{:S(2)}, u32[]{:S(2)}) %collective-permute-start.3) | collective-permute-done | bytes 110624 | tf_op jit(solution)/shard_map/ppermute | solution.py:662
  43.0 3.0 %collective-permute-start.5 = (f32[216,128]{1,0:T(8,128)S(1)}, f32[216,128]{1,0:T(8,128)S(1)}, u32[]{:S(2)}, u32[]{:S(2)}) collective-permute-start(f32[216,128]{1,0:T(8,128)S(1)} %shard_map.84.refs_4_.mine), channel_id=1, source_target_pairs={{0,4},{1,5},{2,6},{3,7},{4,0},{5,1},{6,2},{7,3},{8,12},{9,13},{10,... | collective-permute-start | bytes 331784 | tf_op jit(solution)/shard_map/ppermute | solution.py:662
  46.1 3.4 %collective-permute-start.2 = (bf16[2,32,16,128]{3,2,1,0:T(8,128)(2,1)S(1)}, bf16[2,32,16,128]{3,2,1,0:T(8,128)(2,1)S(1)}, u32[]{:S(2)}, u32[]{:S(2)}) collective-permute-start(bf16[2,32,16,128]{3,2,1,0:T(8,128)(2,1)S(1)} %get-tuple-element.49), channel_id=1, source_target_pairs={{0,1},{1,2},{2,3},{3,4},{4,5},{5,6},{6,7},{7,8},{8,9},{9,10},{10,1... | collective-permute-start | bytes 786440 | tf_op jit(solution)/shard_map/ppermute | solution.py:645
  49.5 1.8 %shard_map.85 = (f32[1,16,8,32,128]{4,3,2,1,0:T(8,128)}, f32[8,128]{1,0:T(8,128)S(1)}) custom-call(bf16[2,128,2304]{2,1,0:T(8,128)(2,1)S(1)} %get-tuple-element.33.mb, bf16[4,34,96,128]{3,2,1,0:T(8,128)(2,1)S(1)} %get-tuple-element.44.refs_0_.refs_1_, ...), custom_call_target="tpu_custom_call", output_to_operand_aliasing={{0}: (6, {})} | custom-call | tf_op jit(solution)/shard_map/pallas_call | solution.py:551
  51.2 0.0 collective-permute-done.5.other
  51.3 2.6 %collective-permute-start.6 = (f32[216,128]{1,0:T(8,128)S(1)}, f32[216,128]{1,0:T(8,128)S(1)}, u32[]{:S(2)}, u32[]{:S(2)}) collective-permute-start(f32[216,128]{1,0:T(8,128)S(1)} %shard_map.86.refs_5_.mine), channel_id=1, source_target_pairs={{0,8},{1,9},{2,10},{3,11},{4,12},{5,13},{6,14},{7,15},{8,0},{9,1},... | collective-permute-start | bytes 331784 | tf_op jit(solution)/shard_map/ppermute | solution.py:662
  53.9 1.8 %shard_map.87 = (f32[1,16,8,32,128]{4,3,2,1,0:T(8,128)}, f32[8,128]{1,0:T(8,128)S(1)}) custom-call(bf16[2,128,2304]{2,1,0:T(8,128)(2,1)S(1)} %get-tuple-element.33.mb, bf16[2,34,96,128]{3,2,1,0:T(8,128)(2,1)S(1)} %get-tuple-element.53.refs_1_.refs_0_, bf16[2,34,96,128]{3,2,1,0:T(8,128)(2,1)S(1)} %get-tuple-element.57.refs_1_, ...), custom_call_target="tpu_custom_call", output_to_operand_aliasing={{0}: (7, {})} | custom-call | tf_op jit(solution)/shard_map/pallas_call | solution.py:551
  55.7 2.0 %collective-permute-done.6.other = f32[216,128]{1,0:T(8,128)S(1)} collective-permute-done((f32[216,128]{1,0:T(8,128)S(1)}, f32[216,128]{1,0:T(8,128)S(1)}, u32[]{:S(2)}, u32[]{:S(2)}) %collective-permute-start.6) | collective-permute-done | bytes 110624 | tf_op jit(solution)/shard_map/ppermute | solution.py:662
  57.7 1.0 %collective-permute-start.7 = (f32[216,128]{1,0:T(8,128)S(1)}, f32[216,128]{1,0:T(8,128)S(1)}, u32[]{:S(2)}, u32[]{:S(2)}) collective-permute-start(f32[216,128]{1,0:T(8,128)S(1)} %shard_map.88.refs_5_.mine), channel_id=1, source_target_pairs={{0,1},{1,0},{2,3},{3,2},{4,5},{5,4},{6,7},{7,6},{8,9},{9,8},{10,11... | collective-permute-start | bytes 331784 | tf_op jit(solution)/shard_map/ppermute | solution.py:662
  58.7 0.0 collective-permute-done.2.refs_4_
  58.7 1.8 %shard_map.89 = (f32[1,16,8,32,128]{4,3,2,1,0:T(8,128)}, f32[8,128]{1,0:T(8,128)S(1)}) custom-call(bf16[2,128,2304]{2,1,0:T(8,128)(2,1)S(1)} %get-tuple-element.33.mb, bf16[2,34,96,128]{3,2,1,0:T(8,128)(2,1)S(1)} %get-tuple-element.40.refs_0_, bf16[4,34,96,128]{3,2,1,0:T(8,128)(2,1)S(1)} %get-tuple-element.44.refs_0_.refs_1_, ...), custom_call_target="tpu_custom_call", output_to_operand_aliasing={{0}: (7, {})} | custom-call | tf_op jit(solution)/shard_map/pallas_call | solution.py:551
  60.5 2.0 %collective-permute-done.7.other = f32[216,128]{1,0:T(8,128)S(1)} collective-permute-done((f32[216,128]{1,0:T(8,128)S(1)}, f32[216,128]{1,0:T(8,128)S(1)}, u32[]{:S(2)}, u32[]{:S(2)}) %collective-permute-start.7) | collective-permute-done | bytes 110624 | tf_op jit(solution)/shard_map/ppermute | solution.py:662
  62.6 0.1 collective-permute-start.8
  62.6 1.3 %collective-permute-done.8.other = f32[216,128]{1,0:T(8,128)S(1)} collective-permute-done((f32[216,128]{1,0:T(8,128)S(1)}, f32[216,128]{1,0:T(8,128)S(1)}, u32[]{:S(2)}, u32[]{:S(2)}) %collective-permute-start.8) | collective-permute-done | bytes 110624 | tf_op jit(solution)/shard_map/ppermute | solution.py:673
  63.9 1.0 %shard_map.91 = f32[2,32,432]{2,1,0:T(8,128)} custom-call(f32[216,128]{1,0:T(8,128)S(1)} %shard_map.90.mine, f32[216,128]{1,0:T(8,128)S(1)} %collective-permute-done.8.other), custom_call_target="tpu_custom_call" | custom-call | bytes 331776 | tf_op jit(solution)/shard_map/pallas_call | solution.py:521
  (5 shorter events, 0.1 us)
Async XLA Ops:
  0.6 1.0 %copy-start = (s32[1,2,8,32,128]{4,3,2,1,0:T(8,128)S(1)}, s32[1,2,8,32,128]{4,3,2,1,0:T(8,128)}, u32[]{:S(2)}) copy-start(s32[1,2,8,32,128]{4,3,2,1,0:T(8,128)} %mask.7) | copy-start | bytes 786436
  1.6 1.2 %copy-start.2 = (bf16[1,16,8,32,128]{4,3,2,1,0:T(8,128)(2,1)S(1)}, bf16[1,16,8,32,128]{4,3,2,1,0:T(8,128)(2,1)}, u32[]{:S(2)}) copy-start(bf16[1,16,8,32,128]{4,3,2,1,0:T(8,128)(2,1)} %vol.3) | copy-start | bytes 3145732
  2.8 17.3 %collective-permute-start = (bf16[33,32,128]{2,1,0:T(8,128)(2,1)S(1)}, bf16[33,32,128]{2,1,0:T(8,128)(2,1)S(1)}, u32[]{:S(2)}, u32[]{:S(2)}) collective-permute-start(bf16[33,32,128]{2,1,0:T(8,128)(2,1)S(1)} %get-tuple-element.34), channel_id=1, source_target_pairs={{0,1},{1,2},{2,3},{3,4},{4,5},{5,6},{6,7},{7,8},{8,9},{9,10},{10,1... | collective-permute-start | bytes 811016 | tf_op jit(solution)/shard_map/ppermute | solution.py:590
  7.7 4.7 %copy-start.1 = (s32[1,2,8,32,128]{4,3,2,1,0:T(8,128)S(1)}, s32[1,2,8,32,128]{4,3,2,1,0:T(8,128)}, u32[]{:S(2)}) copy-start(s32[1,2,8,32,128]{4,3,2,1,0:T(8,128)} %mask.7) | copy-start | bytes 786436
  7.7 4.7 %copy-start.3 = (bf16[1,16,8,32,128]{4,3,2,1,0:T(8,128)(2,1)S(1)}, bf16[1,16,8,32,128]{4,3,2,1,0:T(8,128)(2,1)}, u32[]{:S(2)}) copy-start(bf16[1,16,8,32,128]{4,3,2,1,0:T(8,128)(2,1)} %cot.1) | copy-start | bytes 3145732
  7.7 4.7 %copy-start.4 = (bf16[2,32,432]{2,1,0:T(8,128)(2,1)S(1)}, bf16[2,32,432]{2,1,0:T(8,128)(2,1)}, u32[]{:S(2)}) copy-start(bf16[2,32,432]{2,1,0:T(8,128)(2,1)} %ker.1) | copy-start | bytes 165892
  7.8 21.8 %collective-permute-start.1 = (bf16[33,32,128]{2,1,0:T(8,128)(2,1)S(1)}, bf16[33,32,128]{2,1,0:T(8,128)(2,1)S(1)}, u32[]{:S(2)}, u32[]{:S(2)}) collective-permute-start(bf16[33,32,128]{2,1,0:T(8,128)(2,1)S(1)} %get-tuple-element.47), channel_id=1, source_target_pairs={{1,0},{2,1},{3,2},{4,3},{5,4},{6,5},{7,6},{8,7},{9,8},{10,9},{11,1... | collective-permute-start | bytes 811016 | tf_op jit(solution)/shard_map/ppermute | solution.py:591
  24.0 16.3 %collective-permute-start.4 = (bf16[2,32,16,128]{3,2,1,0:T(8,128)(2,1)S(1)}, bf16[2,32,16,128]{3,2,1,0:T(8,128)(2,1)S(1)}, u32[]{:S(2)}, u32[]{:S(2)}) collective-permute-start(bf16[2,32,16,128]{3,2,1,0:T(8,128)(2,1)S(1)} %get-tuple-element.51), channel_id=1, source_target_pairs={{1,0},{2,1},{3,2},{4,3},{5,4},{6,5},{7,6},{8,7},{9,8},{10,9},{11,1... | collective-permute-start | bytes 786440 | tf_op jit(solution)/shard_map/ppermute | solution.py:629
  35.5 7.5 %collective-permute-start.3 = (f32[216,128]{1,0:T(8,128)S(1)}, f32[216,128]{1,0:T(8,128)S(1)}, u32[]{:S(2)}, u32[]{:S(2)}) collective-permute-start(f32[216,128]{1,0:T(8,128)S(1)} %get-tuple-element.50.refs_2_.mine), channel_id=1, source_target_pairs={{0,2},{1,3},{2,0},{3,1},{4,6},{5,7},{6,4},{7,5},{8,10},{9,11},{10,... | collective-permute-start | bytes 331784 | tf_op jit(solution)/shard_map/ppermute | solution.py:662
  43.0 8.2 %collective-permute-start.5 = (f32[216,128]{1,0:T(8,128)S(1)}, f32[216,128]{1,0:T(8,128)S(1)}, u32[]{:S(2)}, u32[]{:S(2)}) collective-permute-start(f32[216,128]{1,0:T(8,128)S(1)} %shard_map.84.refs_4_.mine), channel_id=1, source_target_pairs={{0,4},{1,5},{2,6},{3,7},{4,0},{5,1},{6,2},{7,3},{8,12},{9,13},{10,... | collective-permute-start | bytes 331784 | tf_op jit(solution)/shard_map/ppermute | solution.py:662
  46.1 12.7 %collective-permute-start.2 = (bf16[2,32,16,128]{3,2,1,0:T(8,128)(2,1)S(1)}, bf16[2,32,16,128]{3,2,1,0:T(8,128)(2,1)S(1)}, u32[]{:S(2)}, u32[]{:S(2)}) collective-permute-start(bf16[2,32,16,128]{3,2,1,0:T(8,128)(2,1)S(1)} %get-tuple-element.49), channel_id=1, source_target_pairs={{0,1},{1,2},{2,3},{3,4},{4,5},{5,6},{6,7},{7,8},{8,9},{9,10},{10,1... | collective-permute-start | bytes 786440 | tf_op jit(solution)/shard_map/ppermute | solution.py:645
  51.3 6.4 %collective-permute-start.6 = (f32[216,128]{1,0:T(8,128)S(1)}, f32[216,128]{1,0:T(8,128)S(1)}, u32[]{:S(2)}, u32[]{:S(2)}) collective-permute-start(f32[216,128]{1,0:T(8,128)S(1)} %shard_map.86.refs_5_.mine), channel_id=1, source_target_pairs={{0,8},{1,9},{2,10},{3,11},{4,12},{5,13},{6,14},{7,15},{8,0},{9,1},... | collective-permute-start | bytes 331784 | tf_op jit(solution)/shard_map/ppermute | solution.py:662
  57.7 4.8 %collective-permute-start.7 = (f32[216,128]{1,0:T(8,128)S(1)}, f32[216,128]{1,0:T(8,128)S(1)}, u32[]{:S(2)}, u32[]{:S(2)}) collective-permute-start(f32[216,128]{1,0:T(8,128)S(1)} %shard_map.88.refs_5_.mine), channel_id=1, source_target_pairs={{0,1},{1,0},{2,3},{3,2},{4,5},{5,4},{6,7},{7,6},{8,9},{9,8},{10,11... | collective-permute-start | bytes 331784 | tf_op jit(solution)/shard_map/ppermute | solution.py:662
  62.6 1.4 %collective-permute-start.8 = (f32[216,128]{1,0:T(8,128)S(1)}, f32[216,128]{1,0:T(8,128)S(1)}, u32[]{:S(2)}, u32[]{:S(2)}) collective-permute-start(f32[216,128]{1,0:T(8,128)S(1)} %shard_map.90.mine), channel_id=1, source_target_pairs={{0,16},{16,0},{1,17},{17,1},{2,18},{18,2},{3,19},{19,3},{4,20},{20... | collective-permute-start | bytes 331784 | tf_op jit(solution)/shard_map/ppermute | solution.py:673

commit v3 on v2

--- a/solution.py
+++ b/solution.py
@@ -324,12 +324,11 @@
     return jnp.where(lane < 2 * outs, both[:half], pltpu.roll(both[half:], 2 * outs, 1))
 
 
-def pack_kernel(vol, mask, up, down):
-    chans, zs = vol.shape[1:3]
-    for out, first, edge in ((up, zs - 2, zs - 1), (down, 0, 0)):
-        for i in range(2):
-            out[i * chans : (i + 1) * chans] = vol[0, :, first + i]
-        out[2 * chans] = mask[0, 0, edge].astype(F32).astype(BF16)
+def pack_kernel(first, edge, vol, mask, *refs):
+    out, chans = refs[-1], vol.shape[1]
+    for i in range(2):
+        out[i * chans : (i + 1) * chans] = vol[0, :, first + i]
+    out[2 * chans] = mask[0, 0, edge].astype(F32).astype(BF16)
 
 
 def arrange_kernel(vol, xv, rows):
@@ -342,19 +341,17 @@
     lax.fori_loop(0, xv.shape[0], arrange, 0)
 
 
-def first_kernel(xv, cot, mask, scale, canary, ker, mf, mb, ct, x1, g1, d2, total, rows, acc):
+def first_kernel(xv, cot, mask, weights, ker, mf, mb, ct, x1, g1, d2, total, rows, acc):
     chans, zs, hs, ws = cot.shape[1:]
     for layer in range(2):
         spread_kernel(ker[layer], mf, layer, 3 * chans, PF)
         spread_kernel(flip_kernel(ker[layer], chans), mb, layer, 6 * chans, PH)
     clear_edges(x1)
     clear_edges(d2)
-    ids = lax.broadcasted_iota(jnp.int32, (chans, ws), 0)
-    weights = jnp.where(ids == canary[...], 3.0, 1.0) * scale[...]
 
     def scaled(z, carry):
         def put(h, t):
-            ct[z, h] = t * weights
+            ct[z, h] = t * weights[...]
 
         to_rows(cot[0, :, z], rows, put)
         return carry
@@ -441,7 +438,7 @@
     total[...] = before[...] + folded(acc, xv.shape[2] // 3)
 
 
-def middle_kernel(xv, g1, ct, mb, d2, before, dx, d1, total, acc):
+def middle_kernel(xv, g1, ct, mb, d2, before, passing, dx, d1, total, passed, acc):
     zs, chans, hs = xv.shape[0], xv.shape[2] // 3, xv.shape[1] - 2
     clear_edges(d1)
     acc[...] = jnp.zeros_like(acc)
@@ -514,10 +511,10 @@
             out[layer, :, part * half : (part + 1) * half] = flat[at : at + outs]
 
 
-def call(body, outs, scratch=(), flops=0, vmem=16 << 20, scalars=(), aliases=()):
+def call(body, outs, scratch=(), flops=0, vmem=16 << 20, aliases=(), outside=()):
     def run(*args):
         size = sum(a.size * a.dtype.itemsize for a in args) + sum(o.size * o.dtype.itemsize for o in outs)
-        spaces = [pltpu.SMEM if i in scalars else VMEM for i in range(len(args))]
+        spaces = [pl.ANY if i in outside else VMEM for i in range(len(args))]
         return pl.pallas_call(
             body,
             out_shape=outs,
@@ -585,10 +582,15 @@
     up = [(i, i + 1) for i in range(peers - 1)]
     down = [(i + 1, i) for i in range(peers - 1)]
 
-    payload = shape(2 * chans + 1, hs, ws, dtype=BF16)
-    going_up, going_down = call(pack_kernel, [payload, payload])(volume, gate_mask)
-    below = lax.ppermute(going_up, "slab", up)
-    above = lax.ppermute(going_down, "slab", down)
+    ids = lax.broadcasted_iota(jnp.int32, (chans, ws), 0)
+    weights = jnp.where(ids == canary, 3.0, 1.0) * loss_scale
+
+    def packed(first, edge, *after):
+        return call_one(
+            functools.partial(pack_kernel, first, edge),
+            shape(2 * chans + 1, hs, ws, dtype=BF16), [],
+            outside=range(2, 2 + len(after)),
+        )(volume, gate_mask, *after)
 
     k_fwd, k_bwd = WZ * (PF + 2) * 3 * chans, WZ * WH * 3 * outs
     m_fwd, m_bwd = PZ * PF * outs, PZ * PH * chans
@@ -601,7 +603,9 @@
     def d_planes(n):
         return shape(n, *d_plane, dtype=BF16)
 
+    below = lax.ppermute(packed(zs - 2, zs - 1, weights), "slab", up)
     (xv,) = call(arrange_kernel, [shape(zs, *x_plane, dtype=BF16)], [rows], flops=pair * 4)(volume)
+    above = lax.ppermute(packed(0, 0, xv), "slab", down)
     mf, mb, ct, x1, g1, d2_in, total_in = call(
         first_kernel,
         [
@@ -615,7 +619,7 @@
         ],
         [rows, acc],
         flops=pair * 6,
-    )(xv, cotangent, gate_mask, loss_scale.reshape((1, 1)), canary.reshape((1, 1)), kernels)
+    )(xv, cotangent, gate_mask, weights, kernels)
 
     halos = [VMEM((2,) + x_plane, BF16), VMEM((2,) + x_plane, BF16)]
     gates = VMEM((2, 2) + c_plane, F32)
@@ -626,13 +630,14 @@
         flops=pair * 5,
         aliases={8: 3},
     )(below, xv, x1, gate_mask, ct, mf, mb, total_in, d2_in)
-    from_above = lax.ppermute(send_lo, "slab", down)
-    dx_in, d1_in, total_in = call(
+    dx_in, d1_in, total_in, send_lo = call(
         middle_kernel,
-        [shape(zs - 4, *c_plane), d_planes(zs - 4), total],
+        [shape(zs - 4, *c_plane), d_planes(zs - 4), total, shape(2, *c_plane, dtype=BF16)],
         [acc],
         flops=pair * 4,
-    )(xv, g1, ct, mb, d2_lo, total_lo)
+        aliases={6: 3},
+    )(xv, g1, ct, mb, d2_lo, total_lo, send_lo)
+    from_above = lax.ppermute(send_lo, "slab", down)
     send_hi, dx_hi, d1_hi, dx_hn, d1_hn, total_hi = call(
         high_kernel,
         [

time: 65.2 us -> 65.3 us (level)
    pallas_call x7 -> x8, Pallas kernels: 24.5 us -> 24.5 us  [run(): pl.pallas_call(body, out_shape=outs, in_specs=[pl.BlockSpec(memory_space=...]
where the time goes in v3:
time: 65.3 us; the launch traced here: 65 us
  Pallas kernels  31.7 us (49%)
  starting transfers between devices  22.7 us (35%)
  waiting for transfers between devices  6.26 us (10%)
  local copies, waits for them, and re-layouts  2.27 us (3%)
  between operations  2.1 us (3%)
    pallas_call x8, Pallas kernels, run(): pl.pallas_call(body, out_shape=outs, in_specs=[pl.BlockSpec(memory_space=...  24.5 us
    ppermute x4, starting transfers between devices, block_device(): other = lax.ppermute(mine, 'slab', [(i, i ^ step) for i in range(peers)])  11.5 us
    pallas_call x4, Pallas kernels, output_planes(): pl.pallas_call(body, grid=(1,), out_shape=[shape(*like.shape), shape(8, w...  7.14 us
    ppermute x4, waiting for transfers between devices, block_device(): other = lax.ppermute(mine, 'slab', [(i, i ^ step) for i in range(peers)])  4.95 us
    ppermute x1, starting transfers between devices, block_device(): below = lax.ppermute(packed(zs - 2, zs - 1, weights), 'slab', up)  4.86 us
    ppermute x1, starting transfers between devices, block_device(): from_below = lax.ppermute(send_hi, 'slab', up)  3.4 us
    unnamed x10, local copies, waits for them, and re-layouts  2.19 us
    ppermute x1, starting transfers between devices, block_device(): from_above = lax.ppermute(send_lo, 'slab', down)  1.47 us
  transfers between devices with their start and end apart: 9, of which 4 were waited for; matrix products, arithmetic and copies ran while one was open for 0% of the time, Pallas kernels for 47%

profile of v3, /device:TPU:0, one launch (start us, length us, event | category | flops | bytes accessed | tf_op | source)
XLA Modules:
  0.0 65.0 jit_solution(1626865008063269920)
XLA Ops:
  1.9 0.1 iota.7.weights.refs_0_
  2.0 0.0 copy-start
  2.0 0.9 %copy-done = s32[1,2,8,32,128]{4,3,2,1,0:T(8,128)S(1)} copy-done((s32[1,2,8,32,128]{4,3,2,1,0:T(8,128)S(1)}, s32[1,2,8,32,128]{4,3,2,1,0:T(8,128)}, u32[]{:S(2)}) %copy-start) | copy-done | bytes 262168
  3.0 0.0 copy-start.2
  3.0 1.2 %copy-done.2 = bf16[1,16,8,32,128]{4,3,2,1,0:T(8,128)(2,1)S(1)} copy-done((bf16[1,16,8,32,128]{4,3,2,1,0:T(8,128)(2,1)S(1)}, bf16[1,16,8,32,128]{4,3,2,1,0:T(8,128)(2,1)}, u32[]{:S(2)}) %copy-start.2) | copy-done | bytes 1048600
  4.2 4.9 %collective-permute-start = (bf16[33,32,128]{2,1,0:T(8,128)(2,1)S(1)}, bf16[33,32,128]{2,1,0:T(8,128)(2,1)S(1)}, u32[]{:S(2)}, u32[]{:S(2)}) collective-permute-start(bf16[33,32,128]{2,1,0:T(8,128)(2,1)S(1)} %shard_map.79), channel_id=1, source_target_pairs={{0,1},{1,2},{2,3},{3,4},{4,5},{5,6},{6,7},{7,8},{8,9},{9,10},{10,1... | collective-permute-start | bytes 811016 | tf_op jit(solution)/shard_map/ppermute | solution.py:606
  9.1 1.9 %shard_map.77.xv.refs_0_ = bf16[8,34,48,128]{3,2,1,0:T(8,128)(2,1)S(1)} custom-call(bf16[1,16,8,32,128]{4,3,2,1,0:T(8,128)(2,1)S(1)} %copy-done.2), custom_call_target="tpu_custom_call" | custom-call | flops 2415919104 | bytes 4390912 | tf_op jit(solution)/shard_map/pallas_call | solution.py:518
  11.0 0.0 copy-start.1
  11.0 0.0 copy-start.3
  11.0 0.0 copy-start.4
  11.1 1.4 %collective-permute-start.1 = (bf16[33,32,128]{2,1,0:T(8,128)(2,1)S(1)}, bf16[33,32,128]{2,1,0:T(8,128)(2,1)S(1)}, u32[]{:S(2)}, u32[]{:S(2)}) collective-permute-start(bf16[33,32,128]{2,1,0:T(8,128)(2,1)S(1)} %shard_map.82), channel_id=1, source_target_pairs={{1,0},{2,1},{3,2},{4,3},{5,4},{6,5},{7,6},{8,7},{9,8},{10,9},{11,1... | collective-permute-start | bytes 811016 | tf_op jit(solution)/shard_map/ppermute | solution.py:608
  12.5 0.0 copy-done.1
  12.5 0.0 copy-done.3
  12.5 0.0 copy-done.4
  12.5 7.7 %shard_map.78 = (bf16[2,128,768]{2,1,0:T(8,128)(2,1)S(1)}, bf16[2,128,2304]{2,1,0:T(8,128)(2,1)S(1)}, f32[8,32,16,128]{3,2,1,0:T(8,128)S(1)}, bf16[6,34,48,128]{...) custom-call(bf16[8,34,48,128]{3,2,1,0:T(8,128)(2,1)S(1)} %shard_map., ...), custom_call_target="tpu_custom_call" | custom-call | flops 3623878656 | bytes 19163136 | tf_op jit(solution)/shard_map/pallas_call | solution.py:518
  20.3 0.0 collective-permute-done.halo
  20.3 3.8 %shard_map.80 = (bf16[2,32,16,128]{3,2,1,0:T(8,128)(2,1)S(1)}, f32[2,32,16,128]{3,2,1,0:T(8,128)S(1)}, bf16[2,34,96,128]{3,2,1,0:T(8,128)(2,1)S(1)}, bf16[6,34,96,128]{3,2,1,0:T(8,128)(2,1)S(1)}, f32[216,128]{1,0:T(8,128)S(1)}) custom-call(bf16[33,32,128]{2,1,0:T(8,128)(2,1)S(1)} %collective-permute-done.halo, ...), custom_call_target="tpu_custom_call", output_to_operand_aliasing={{3}: (8, {})} | custom-call | flops 3019898880 | bytes 22757376 | tf_op jit(solution)/shard_map/pallas_call | solution.py:518
  24.1 4.0 %shard_map.81 = (f32[4,32,16,128]{3,2,1,0:T(8,128)S(1)}, bf16[4,34,96,128]{3,2,1,0:T(8,128)(2,1)S(1)}, f32[216,128]{1,0:T(8,128)S(1)}, bf16[2,32,16,128]{3,2,1,0:T(8,128)(2,1)S(1)}) custom-call(bf16[8,34,48,128]{3,2,1,0:T(8,128)(2,1)S(1)} %shard_map.77.xv.refs_0_, f32[2,6,32,16,128]{4,3,2,1,0:T(8,128)S(1)} %get-tuple-element.39.g1, ...), custom_call_target="tpu_custom_call", output_to_operand_aliasing={{3}: (6, {})} | custom-call | flops 2415919104 | bytes 19914752 | tf_op jit(solution)/shard_map/pallas_call | solution.py:518
  28.1 1.5 %collective-permute-start.4 = (bf16[2,32,16,128]{3,2,1,0:T(8,128)(2,1)S(1)}, bf16[2,32,16,128]{3,2,1,0:T(8,128)(2,1)S(1)}, u32[]{:S(2)}, u32[]{:S(2)}) collective-permute-start(bf16[2,32,16,128]{3,2,1,0:T(8,128)(2,1)S(1)} %get-tuple-element.49), channel_id=1, source_target_pairs={{1,0},{2,1},{3,2},{4,3},{5,4},{6,5},{7,6},{8,7},{9,8},{10,9},{11,1... | collective-permute-start | bytes 786440 | tf_op jit(solution)/shard_map/ppermute | solution.py:640
  29.6 0.0 collective-permute-done.1.halo
  29.6 6.0 %shard_map.83 = (bf16[2,32,16,128]{3,2,1,0:T(8,128)(2,1)S(1)}, f32[2,32,16,128]{3,2,1,0:T(8,128)S(1)}, bf16[2,34,96,128]{3,2,1,0:T(8,128)(2,1)S(1)}, f32[2,32,16...) custom-call(bf16[33,32,128]{2,1,0:T(8,128)(2,1)S(1)} %collective-permute-done.1.halo, ...), custom_call_target="tpu_custom_call" | custom-call | flops 4227858432 | bytes 23085056 | tf_op jit(solution)/shard_map/pallas_call | solution.py:518
  35.6 4.8 %collective-permute-start.3 = (f32[216,128]{1,0:T(8,128)S(1)}, f32[216,128]{1,0:T(8,128)S(1)}, u32[]{:S(2)}, u32[]{:S(2)}) collective-permute-start(f32[216,128]{1,0:T(8,128)S(1)} %get-tuple-element.48.refs_2_.mine), channel_id=1, source_target_pairs={{0,2},{1,3},{2,0},{3,1},{4,6},{5,7},{6,4},{7,5},{8,10},{9,11},{10,... | collective-permute-start | bytes 331784 | tf_op jit(solution)/shard_map/ppermute | solution.py:667
  40.4 0.0 collective-permute-done.4.refs_3_.refs_4_
  40.4 1.8 %shard_map.84 = (f32[1,16,8,32,128]{4,3,2,1,0:T(8,128)}, f32[8,128]{1,0:T(8,128)S(1)}) custom-call(bf16[2,128,2304]{2,1,0:T(8,128)(2,1)S(1)} %get-tuple-element.32.mb, bf16[4,34,96,128]{3,2,1,0:T(8,128)(2,1)S(1)} %get-tuple-element.43.refs_0_.refs_1_, f32[4,32,16,128]{3,2,1,0:T(8,128)S(1)} %get-tuple-element.45.refs_1_.refs_2_.refs_3_, ...), custom_call_target="tpu_custom_call" | custom-call | tf_op jit(solution)/shard_map/pallas_call | solution.py:548
  42.2 1.0 %collective-permute-done.3.other = f32[216,128]{1,0:T(8,128)S(1)} collective-permute-done((f32[216,128]{1,0:T(8,128)S(1)}, f32[216,128]{1,0:T(8,128)S(1)}, u32[]{:S(2)}, u32[]{:S(2)}) %collective-permute-start.3) | collective-permute-done | bytes 110624 | tf_op jit(solution)/shard_map/ppermute | solution.py:667
  43.1 3.0 %collective-permute-start.5 = (f32[216,128]{1,0:T(8,128)S(1)}, f32[216,128]{1,0:T(8,128)S(1)}, u32[]{:S(2)}, u32[]{:S(2)}) collective-permute-start(f32[216,128]{1,0:T(8,128)S(1)} %shard_map.85.refs_4_.mine), channel_id=1, source_target_pairs={{0,4},{1,5},{2,6},{3,7},{4,0},{5,1},{6,2},{7,3},{8,12},{9,13},{10,... | collective-permute-start | bytes 331784 | tf_op jit(solution)/shard_map/ppermute | solution.py:667
  46.2 3.4 %collective-permute-start.2 = (bf16[2,32,16,128]{3,2,1,0:T(8,128)(2,1)S(1)}, bf16[2,32,16,128]{3,2,1,0:T(8,128)(2,1)S(1)}, u32[]{:S(2)}, u32[]{:S(2)}) collective-permute-start(bf16[2,32,16,128]{3,2,1,0:T(8,128)(2,1)S(1)} %get-tuple-element.47), channel_id=1, source_target_pairs={{0,1},{1,2},{2,3},{3,4},{4,5},{5,6},{6,7},{7,8},{8,9},{9,10},{10,1... | collective-permute-start | bytes 786440 | tf_op jit(solution)/shard_map/ppermute | solution.py:650
  49.6 1.8 %shard_map.86 = (f32[1,16,8,32,128]{4,3,2,1,0:T(8,128)}, f32[8,128]{1,0:T(8,128)S(1)}) custom-call(bf16[2,128,2304]{2,1,0:T(8,128)(2,1)S(1)} %get-tuple-element.32.mb, bf16[4,34,96,128]{3,2,1,0:T(8,128)(2,1)S(1)} %get-tuple-element.43.refs_0_.refs_1_, ...), custom_call_target="tpu_custom_call", output_to_operand_aliasing={{0}: (6, {})} | custom-call | tf_op jit(solution)/shard_map/pallas_call | solution.py:548
  51.3 0.0 collective-permute-done.5.other
  51.4 2.6 %collective-permute-start.6 = (f32[216,128]{1,0:T(8,128)S(1)}, f32[216,128]{1,0:T(8,128)S(1)}, u32[]{:S(2)}, u32[]{:S(2)}) collective-permute-start(f32[216,128]{1,0:T(8,128)S(1)} %shard_map.87.refs_5_.mine), channel_id=1, source_target_pairs={{0,8},{1,9},{2,10},{3,11},{4,12},{5,13},{6,14},{7,15},{8,0},{9,1},... | collective-permute-start | bytes 331784 | tf_op jit(solution)/shard_map/ppermute | solution.py:667
  54.0 1.8 %shard_map.88 = (f32[1,16,8,32,128]{4,3,2,1,0:T(8,128)}, f32[8,128]{1,0:T(8,128)S(1)}) custom-call(bf16[2,128,2304]{2,1,0:T(8,128)(2,1)S(1)} %get-tuple-element.32.mb, bf16[2,34,96,128]{3,2,1,0:T(8,128)(2,1)S(1)} %get-tuple-element.51.refs_1_.refs_0_, bf16[2,34,96,128]{3,2,1,0:T(8,128)(2,1)S(1)} %get-tuple-element.55.refs_1_, ...), custom_call_target="tpu_custom_call", output_to_operand_aliasing={{0}: (7, {})} | custom-call | tf_op jit(solution)/shard_map/pallas_call | solution.py:548
  55.8 2.0 %collective-permute-done.6.other = f32[216,128]{1,0:T(8,128)S(1)} collective-permute-done((f32[216,128]{1,0:T(8,128)S(1)}, f32[216,128]{1,0:T(8,128)S(1)}, u32[]{:S(2)}, u32[]{:S(2)}) %collective-permute-start.6) | collective-permute-done | bytes 110624 | tf_op jit(solution)/shard_map/ppermute | solution.py:667
  57.8 1.0 %collective-permute-start.7 = (f32[216,128]{1,0:T(8,128)S(1)}, f32[216,128]{1,0:T(8,128)S(1)}, u32[]{:S(2)}, u32[]{:S(2)}) collective-permute-start(f32[216,128]{1,0:T(8,128)S(1)} %shard_map.89.refs_5_.mine), channel_id=1, source_target_pairs={{0,1},{1,0},{2,3},{3,2},{4,5},{5,4},{6,7},{7,6},{8,9},{9,8},{10,11... | collective-permute-start | bytes 331784 | tf_op jit(solution)/shard_map/ppermute | solution.py:667
  58.8 0.0 collective-permute-done.2.refs_4_
  58.8 1.8 %shard_map.90 = (f32[1,16,8,32,128]{4,3,2,1,0:T(8,128)}, f32[8,128]{1,0:T(8,128)S(1)}) custom-call(bf16[2,128,2304]{2,1,0:T(8,128)(2,1)S(1)} %get-tuple-element.32.mb, bf16[2,34,96,128]{3,2,1,0:T(8,128)(2,1)S(1)} %get-tuple-element.38.refs_0_, bf16[4,34,96,128]{3,2,1,0:T(8,128)(2,1)S(1)} %get-tuple-element.43.refs_0_.refs_1_, ...), custom_call_target="tpu_custom_call", output_to_operand_aliasing={{0}: (7, {})} | custom-call | tf_op jit(solution)/shard_map/pallas_call | solution.py:548
  60.6 2.0 %collective-permute-done.7.other = f32[216,128]{1,0:T(8,128)S(1)} collective-permute-done((f32[216,128]{1,0:T(8,128)S(1)}, f32[216,128]{1,0:T(8,128)S(1)}, u32[]{:S(2)}, u32[]{:S(2)}) %collective-permute-start.7) | collective-permute-done | bytes 110624 | tf_op jit(solution)/shard_map/ppermute | solution.py:667
  62.7 0.1 collective-permute-start.8
  62.7 1.3 %collective-permute-done.8.other = f32[216,128]{1,0:T(8,128)S(1)} collective-permute-done((f32[216,128]{1,0:T(8,128)S(1)}, f32[216,128]{1,0:T(8,128)S(1)}, u32[]{:S(2)}, u32[]{:S(2)}) %collective-permute-start.8) | collective-permute-done | bytes 110624 | tf_op jit(solution)/shard_map/ppermute | solution.py:678
  64.0 1.0 %shard_map.92 = f32[2,32,432]{2,1,0:T(8,128)} custom-call(f32[216,128]{1,0:T(8,128)S(1)} %shard_map.91.mine, f32[216,128]{1,0:T(8,128)S(1)} %collective-permute-done.8.other), custom_call_target="tpu_custom_call" | custom-call | bytes 331776 | tf_op jit(solution)/shard_map/pallas_call | solution.py:518
  (7 shorter events, 0.1 us)
Async XLA Ops:
  2.0 1.0 %copy-start = (s32[1,2,8,32,128]{4,3,2,1,0:T(8,128)S(1)}, s32[1,2,8,32,128]{4,3,2,1,0:T(8,128)}, u32[]{:S(2)}) copy-start(s32[1,2,8,32,128]{4,3,2,1,0:T(8,128)} %mask.9) | copy-start | bytes 786436
  3.0 1.2 %copy-start.2 = (bf16[1,16,8,32,128]{4,3,2,1,0:T(8,128)(2,1)S(1)}, bf16[1,16,8,32,128]{4,3,2,1,0:T(8,128)(2,1)}, u32[]{:S(2)}) copy-start(bf16[1,16,8,32,128]{4,3,2,1,0:T(8,128)(2,1)} %vol.5) | copy-start | bytes 3145732
  4.2 16.1 %collective-permute-start = (bf16[33,32,128]{2,1,0:T(8,128)(2,1)S(1)}, bf16[33,32,128]{2,1,0:T(8,128)(2,1)S(1)}, u32[]{:S(2)}, u32[]{:S(2)}) collective-permute-start(bf16[33,32,128]{2,1,0:T(8,128)(2,1)S(1)} %shard_map.79), channel_id=1, source_target_pairs={{0,1},{1,2},{2,3},{3,4},{4,5},{5,6},{6,7},{7,8},{8,9},{9,10},{10,1... | collective-permute-start | bytes 811016 | tf_op jit(solution)/shard_map/ppermute | solution.py:606
  11.0 1.5 %copy-start.1 = (s32[1,2,8,32,128]{4,3,2,1,0:T(8,128)S(1)}, s32[1,2,8,32,128]{4,3,2,1,0:T(8,128)}, u32[]{:S(2)}) copy-start(s32[1,2,8,32,128]{4,3,2,1,0:T(8,128)} %mask.9) | copy-start | bytes 786436
  11.0 1.5 %copy-start.3 = (bf16[1,16,8,32,128]{4,3,2,1,0:T(8,128)(2,1)S(1)}, bf16[1,16,8,32,128]{4,3,2,1,0:T(8,128)(2,1)}, u32[]{:S(2)}) copy-start(bf16[1,16,8,32,128]{4,3,2,1,0:T(8,128)(2,1)} %cot.1) | copy-start | bytes 3145732
  11.0 1.5 %copy-start.4 = (bf16[2,32,432]{2,1,0:T(8,128)(2,1)S(1)}, bf16[2,32,432]{2,1,0:T(8,128)(2,1)}, u32[]{:S(2)}) copy-start(bf16[2,32,432]{2,1,0:T(8,128)(2,1)} %ker.1) | copy-start | bytes 165892
  11.1 18.6 %collective-permute-start.1 = (bf16[33,32,128]{2,1,0:T(8,128)(2,1)S(1)}, bf16[33,32,128]{2,1,0:T(8,128)(2,1)S(1)}, u32[]{:S(2)}, u32[]{:S(2)}) collective-permute-start(bf16[33,32,128]{2,1,0:T(8,128)(2,1)S(1)} %shard_map.82), channel_id=1, source_target_pairs={{1,0},{2,1},{3,2},{4,3},{5,4},{6,5},{7,6},{8,7},{9,8},{10,9},{11,1... | collective-permute-start | bytes 811016 | tf_op jit(solution)/shard_map/ppermute | solution.py:608
  28.1 12.2 %collective-permute-start.4 = (bf16[2,32,16,128]{3,2,1,0:T(8,128)(2,1)S(1)}, bf16[2,32,16,128]{3,2,1,0:T(8,128)(2,1)S(1)}, u32[]{:S(2)}, u32[]{:S(2)}) collective-permute-start(bf16[2,32,16,128]{3,2,1,0:T(8,128)(2,1)S(1)} %get-tuple-element.49), channel_id=1, source_target_pairs={{1,0},{2,1},{3,2},{4,3},{5,4},{6,5},{7,6},{8,7},{9,8},{10,9},{11,1... | collective-permute-start | bytes 786440 | tf_op jit(solution)/shard_map/ppermute | solution.py:640
  35.6 7.5 %collective-permute-start.3 = (f32[216,128]{1,0:T(8,128)S(1)}, f32[216,128]{1,0:T(8,128)S(1)}, u32[]{:S(2)}, u32[]{:S(2)}) collective-permute-start(f32[216,128]{1,0:T(8,128)S(1)} %get-tuple-element.48.refs_2_.mine), channel_id=1, source_target_pairs={{0,2},{1,3},{2,0},{3,1},{4,6},{5,7},{6,4},{7,5},{8,10},{9,11},{10,... | collective-permute-start | bytes 331784 | tf_op jit(solution)/shard_map/ppermute | solution.py:667
  43.1 8.2 %collective-permute-start.5 = (f32[216,128]{1,0:T(8,128)S(1)}, f32[216,128]{1,0:T(8,128)S(1)}, u32[]{:S(2)}, u32[]{:S(2)}) collective-permute-start(f32[216,128]{1,0:T(8,128)S(1)} %shard_map.85.refs_4_.mine), channel_id=1, source_target_pairs={{0,4},{1,5},{2,6},{3,7},{4,0},{5,1},{6,2},{7,3},{8,12},{9,13},{10,... | collective-permute-start | bytes 331784 | tf_op jit(solution)/shard_map/ppermute | solution.py:667
  46.2 12.7 %collective-permute-start.2 = (bf16[2,32,16,128]{3,2,1,0:T(8,128)(2,1)S(1)}, bf16[2,32,16,128]{3,2,1,0:T(8,128)(2,1)S(1)}, u32[]{:S(2)}, u32[]{:S(2)}) collective-permute-start(bf16[2,32,16,128]{3,2,1,0:T(8,128)(2,1)S(1)} %get-tuple-element.47), channel_id=1, source_target_pairs={{0,1},{1,2},{2,3},{3,4},{4,5},{5,6},{6,7},{7,8},{8,9},{9,10},{10,1... | collective-permute-start | bytes 786440 | tf_op jit(solution)/shard_map/ppermute | solution.py:650
  51.4 6.4 %collective-permute-start.6 = (f32[216,128]{1,0:T(8,128)S(1)}, f32[216,128]{1,0:T(8,128)S(1)}, u32[]{:S(2)}, u32[]{:S(2)}) collective-permute-start(f32[216,128]{1,0:T(8,128)S(1)} %shard_map.87.refs_5_.mine), channel_id=1, source_target_pairs={{0,8},{1,9},{2,10},{3,11},{4,12},{5,13},{6,14},{7,15},{8,0},{9,1},... | collective-permute-start | bytes 331784 | tf_op jit(solution)/shard_map/ppermute | solution.py:667
  57.8 4.8 %collective-permute-start.7 = (f32[216,128]{1,0:T(8,128)S(1)}, f32[216,128]{1,0:T(8,128)S(1)}, u32[]{:S(2)}, u32[]{:S(2)}) collective-permute-start(f32[216,128]{1,0:T(8,128)S(1)} %shard_map.89.refs_5_.mine), channel_id=1, source_target_pairs={{0,1},{1,0},{2,3},{3,2},{4,5},{5,4},{6,7},{7,6},{8,9},{9,8},{10,11... | collective-permute-start | bytes 331784 | tf_op jit(solution)/shard_map/ppermute | solution.py:667
  62.7 1.4 %collective-permute-start.8 = (f32[216,128]{1,0:T(8,128)S(1)}, f32[216,128]{1,0:T(8,128)S(1)}, u32[]{:S(2)}, u32[]{:S(2)}) collective-permute-start(f32[216,128]{1,0:T(8,128)S(1)} %shard_map.91.mine), channel_id=1, source_target_pairs={{0,16},{16,0},{1,17},{17,1},{2,18},{18,2},{3,19},{19,3},{4,20},{20... | collective-permute-start | bytes 331784 | tf_op jit(solution)/shard_map/ppermute | solution.py:678
